TPU v7x, 512 devices: a whole 4x8x8 slice. The times are simulated.
512 devices in a mesh: stream: 16 (over z, core), span: 32 (over x, y).
Axes of the slice: x: 4, y: 8, z: 8, core: 2. Of those that a mesh axis runs over, the one named last changes fastest.
Arguments:
- right_side: bfloat16 [16, 1792, 1600], P('stream', 'span'), may hold values from -2.390625 to 2.390625
- up_blocks: bfloat16 [16, 1792, 20000], P('stream', 'span'), may hold values from -0.375 to 0.375
- inverses: bfloat16 [16, 1792, 10000], P('stream', 'span'), may hold values from -0.625 to 0.625
- up_cells: int32 [16, 1792, 2], P('stream', 'span'), may hold values from 0 to 27
- piece_rhs: bfloat16 [16, 1536, 1600], P('stream', 'span'), may hold values from -2.390625 to 2.390625
- piece_blocks: bfloat16 [16, 1536, 10000], P('stream', 'span'), may hold values from -0.375 to 0.375
- piece_up: int32 [16, 1536], P('stream', 'span'), may hold values from 0 to 27
- piece_owner: int32 [16, 1536, 1], P('stream', 'span'), may hold values from 0 to 31; in each aligned block of 24 rows (0 to 23, 24 to 47, ..., all dimensions but the last counted through in order) at most 2 rows name the same one
- piece_cell: int32 [16, 1536], P('stream', 'span'), may hold values from 0 to 27
Outputs:
- sweep_states: bfloat16 [16, 1792, 1600], P('stream', 'span')
Inputs may be any that keep to these rules, and one draw needn't show every extreme that they name: `up_cells`: each upstream cell is on the device of the same span index in the previous section and in the same sweep group. `piece_up`: the upstream cell of a piece is on the device of the same span index in the previous section and in the piece's sweep group. `piece_owner`: among the rows of one device in one sweep group (aligned blocks of 24 rows), at most 2 name the same owner device; some device and group reach 2. `piece_cell`: the owner cell is in the piece's sweep group on the owner device.
All inputs are finite; a program needn't handle non-finite values.
Results may differ from a plain program's by a relative error of at most 0.035.
Values may be sent and summed in bfloat16 or wider, within the bound.
A program may use at most 64 MiB of HBM per device.

v0:
```python
import jax
import jax.numpy as jnp
from jax import lax
from jax.sharding import PartitionSpec as P

U = 100
R = 16
CELLS = 56
SLOTS = 48
GROUPS = 2


def passed_along(value, axis, steps):
    count = lax.axis_size(axis)
    leading, last = (max(0, -steps), min(count, count - steps))
    return lax.ppermute(value, axis, [(source, source + steps) for source in range(leading, last)])


def owner_terms(upstream, upstream_links, face_blocks, cell_rhs):
    nearby = upstream[upstream_links]
    coupled = jnp.einsum("nkij,nkjr->nir", face_blocks, nearby, preferred_element_type=jnp.float32)
    return cell_rhs.astype(jnp.float32) - coupled


def piece_terms(upstream, upstream_links, face_blocks, cell_rhs):
    nearby = upstream[upstream_links]
    coupled = jnp.einsum("nij,njr->nir", face_blocks, nearby, preferred_element_type=jnp.float32)
    return (cell_rhs.astype(jnp.float32) - coupled).astype(jnp.bfloat16)


def apply_inverse(merged, inverse_blocks):
    return jnp.einsum(
        "nij,njr->nir", inverse_blocks, merged, preferred_element_type=jnp.float32
    ).astype(jnp.bfloat16)


def on_device(
    right_side,
    up_blocks,
    inverses,
    up_cells,
    piece_rhs,
    piece_blocks,
    piece_up,
    piece_owner,
    piece_cell,
):
    span_count = lax.axis_size("span")
    section_count = lax.axis_size("stream")
    cell_grp = CELLS // GROUPS
    slot_grp = SLOTS // GROUPS
    capacity = max(2, 2 * slot_grp // span_count)
    cell_rhs = right_side[0].reshape(CELLS, U, R)
    face_blocks = up_blocks[0].reshape(CELLS, 2, U, U)
    inverse_blocks = inverses[0].reshape(CELLS, U, U)
    face_links = up_cells[0]
    pieces_rhs = piece_rhs[0].reshape(SLOTS, U, R)
    pieces_blocks = piece_blocks[0].reshape(SLOTS, U, U)
    pieces_up = piece_up[0]
    pieces_dest = piece_owner[0, :, 0]
    pieces_cell = piece_cell[0]
    cell_group = jnp.arange(CELLS, dtype=jnp.int32) // cell_grp * cell_grp
    piece_group = jnp.arange(SLOTS, dtype=jnp.int32) // slot_grp
    dest_onehot = (pieces_dest[:, None] == jnp.arange(span_count, dtype=jnp.int32)[None, :]).astype(
        jnp.int32
    )
    grouped = dest_onehot.reshape(GROUPS, slot_grp, span_count)
    earlier = jnp.cumsum(grouped, axis=1) - grouped
    slot_rank = jnp.sum(earlier * grouped, axis=2).reshape(SLOTS)
    width = GROUPS * capacity
    position = pieces_dest * width + piece_group * capacity + slot_rank
    index_table = (
        jnp.full((span_count * width,), -1, jnp.int32)
        .at[position]
        .set(piece_group * cell_grp + pieces_cell)
    )
    arrivals = lax.all_to_all(
        index_table.reshape(span_count, width), "span", split_axis=0, concat_axis=0, tiled=True
    )
    selector = (
        arrivals.reshape(-1)[None, :] == jnp.arange(CELLS, dtype=jnp.int32)[:, None]
    ).astype(jnp.bfloat16)
    cell_links = cell_group[:, None] + face_links
    piece_links = piece_group * cell_grp + pieces_up

    def section_turn(turn, states):
        upstream = passed_along(states, "stream", 1)
        owned = owner_terms(upstream, cell_links, face_blocks, cell_rhs)
        partial_value = piece_terms(upstream, piece_links, pieces_blocks, pieces_rhs)
        outbox = (
            jnp.zeros((span_count * width, U * R), jnp.bfloat16)
            .at[position]
            .set(partial_value.reshape(SLOTS, U * R))
        )
        inbox = lax.all_to_all(
            outbox.reshape(span_count, width, U * R),
            "span",
            split_axis=0,
            concat_axis=0,
            tiled=True,
        )
        summed = jnp.dot(
            selector, inbox.reshape(span_count * width, U * R), preferred_element_type=jnp.float32
        )
        merged = (owned + summed.reshape(CELLS, U, R)).astype(jnp.bfloat16)
        return apply_inverse(merged, inverse_blocks)

    states = lax.fori_loop(0, section_count, section_turn, jnp.zeros((CELLS, U, R), jnp.bfloat16))
    return states.reshape(1, CELLS, U * R)


def solution(mesh):
    in_specs = (
        P("stream", "span", None),
        P("stream", "span", None),
        P("stream", "span", None),
        P("stream", "span", None),
        P("stream", "span", None),
        P("stream", "span", None),
        P("stream", "span"),
        P("stream", "span", None),
        P("stream", "span"),
    )
    out_specs = P("stream", "span", None)
    return jax.shard_map(
        on_device, mesh=mesh, in_specs=in_specs, out_specs=out_specs, check_vma=False
    )
```

profile of v0, /device:TPU:72, one launch (start us, length us, event | category | flops | bytes accessed | tf_op | source)
XLA Modules:
  0.0 638.8 jit_solution(6778669483046844193)
XLA Ops:
  5.8 10.2 %all-to-all-start.1 = ((s32[32,1,4]{2,1,0:T(1,128)}), s32[32,1,4]{2,1,0:T(1,128)S(1)}, u32[]{:S(2)}, u32[]{:S(2)}) async-start(s32[32,1,4]{2,1,0:T(1,128)} %bitcast.8), calls=%async_computation.1 | async-start | bytes 32768 | tf_op jit(solution)/shard_map/all_to_all | solution.py:77
  16.7 7.9 %reshape_squeeze.16 = bf16[56,2,100,100]{3,2,1,0:T(8,128)(2,1)} reshape(bf16[1,56,20000]{2,1,0:T(8,128)(2,1)} %param.12) | data formatting | bytes 4480000 | tf_op jit(solution)/shard_map/reshape;squeeze | solution.py:54
  34.2 602.4 %while.11 = (s32[]{:T(128)}, bf16[56,100,16]{1,2,0:T(8,128)(2,1)}, bf16[56,100,16]{1,2,0:T(8,128)(2,1)}, s32[56,2]{0,1:T(2,128)S(1)}, bf16[56,2,100,100]{3,2,1,0...) while((s32[]{:T(128)}, bf16[56,100,16]{1,2,0:T(8,128)(2,1)}, ...), condition=%wide.region_5.6_spmd.clone, body=%wide.region_3.5_spmd.clone.sunk | while | flops 92753008 | bytes 14452835 | solution.py:108
  36.1 5.6 collective-permute-done
  46.9 9.8 %all-to-all-start = ((bf16[32,4,1600]{2,1,0:T(4,128)(2,1)}), bf16[32,4,1600]{2,1,0:T(4,128)(2,1)S(1)}, u32[]{:S(2)}, u32[]{:S(2)}) async-start(bf16[32,4,1600]{2,1,0:T(4,128)(2,1)} %reshape.257), calls=%async_computation | async-start | bytes 851968 | tf_op jit(solution)/shard_map/while/body/eval_jaxpr/all_to_all | solution.py:95
  57.7 14.9 %all-to-all-done = bf16[32,4,1600]{2,1,0:T(4,128)(2,1)S(1)} async-done(((bf16[32,4,1600]{2,1,0:T(4,128)(2,1)}), bf16[32,4,1600]{2,1,0:T(4,128)(2,1)S(1)}, u32[]{:S(2)}, u32[]{:S(2)}) %all-to-all-start) | async-done | bytes 409632 | tf_op jit(solution)/shard_map/while/body/eval_jaxpr/all_to_all | solution.py:95
  79.9 5.6 collective-permute-done
  96.5 14.9 %all-to-all-done = bf16[32,4,1600]{2,1,0:T(4,128)(2,1)S(1)} async-done(((bf16[32,4,1600]{2,1,0:T(4,128)(2,1)}), bf16[32,4,1600]{2,1,0:T(4,128)(2,1)S(1)}, u32[]{:S(2)}, u32[]{:S(2)}) %all-to-all-start) | async-done | bytes 409632 | tf_op jit(solution)/shard_map/while/body/eval_jaxpr/all_to_all | solution.py:95
  118.7 5.6 collective-permute-done
  135.3 15.7 %all-to-all-done = bf16[32,4,1600]{2,1,0:T(4,128)(2,1)S(1)} async-done(((bf16[32,4,1600]{2,1,0:T(4,128)(2,1)}), bf16[32,4,1600]{2,1,0:T(4,128)(2,1)S(1)}, u32[]{:S(2)}, u32[]{:S(2)}) %all-to-all-start) | async-done | bytes 409632 | tf_op jit(solution)/shard_map/while/body/eval_jaxpr/all_to_all | solution.py:95
  175.2 14.1 %all-to-all-done = bf16[32,4,1600]{2,1,0:T(4,128)(2,1)S(1)} async-done(((bf16[32,4,1600]{2,1,0:T(4,128)(2,1)}), bf16[32,4,1600]{2,1,0:T(4,128)(2,1)S(1)}, u32[]{:S(2)}, u32[]{:S(2)}) %all-to-all-start) | async-done | bytes 409632 | tf_op jit(solution)/shard_map/while/body/eval_jaxpr/all_to_all | solution.py:95
  213.2 14.1 %all-to-all-done = bf16[32,4,1600]{2,1,0:T(4,128)(2,1)S(1)} async-done(((bf16[32,4,1600]{2,1,0:T(4,128)(2,1)}), bf16[32,4,1600]{2,1,0:T(4,128)(2,1)S(1)}, u32[]{:S(2)}, u32[]{:S(2)}) %all-to-all-start) | async-done | bytes 409632 | tf_op jit(solution)/shard_map/while/body/eval_jaxpr/all_to_all | solution.py:95
  251.1 14.1 %all-to-all-done = bf16[32,4,1600]{2,1,0:T(4,128)(2,1)S(1)} async-done(((bf16[32,4,1600]{2,1,0:T(4,128)(2,1)}), bf16[32,4,1600]{2,1,0:T(4,128)(2,1)S(1)}, u32[]{:S(2)}, u32[]{:S(2)}) %all-to-all-start) | async-done | bytes 409632 | tf_op jit(solution)/shard_map/while/body/eval_jaxpr/all_to_all | solution.py:95
  289.0 12.9 %all-to-all-done = bf16[32,4,1600]{2,1,0:T(4,128)(2,1)S(1)} async-done(((bf16[32,4,1600]{2,1,0:T(4,128)(2,1)}), bf16[32,4,1600]{2,1,0:T(4,128)(2,1)S(1)}, u32[]{:S(2)}, u32[]{:S(2)}) %all-to-all-start) | async-done | bytes 409632 | tf_op jit(solution)/shard_map/while/body/eval_jaxpr/all_to_all | solution.py:95
  325.7 12.8 %all-to-all-done = bf16[32,4,1600]{2,1,0:T(4,128)(2,1)S(1)} async-done(((bf16[32,4,1600]{2,1,0:T(4,128)(2,1)}), bf16[32,4,1600]{2,1,0:T(4,128)(2,1)S(1)}, u32[]{:S(2)}, u32[]{:S(2)}) %all-to-all-start) | async-done | bytes 409632 | tf_op jit(solution)/shard_map/while/body/eval_jaxpr/all_to_all | solution.py:95
  362.3 12.8 %all-to-all-done = bf16[32,4,1600]{2,1,0:T(4,128)(2,1)S(1)} async-done(((bf16[32,4,1600]{2,1,0:T(4,128)(2,1)}), bf16[32,4,1600]{2,1,0:T(4,128)(2,1)S(1)}, u32[]{:S(2)}, u32[]{:S(2)}) %all-to-all-start) | async-done | bytes 409632 | tf_op jit(solution)/shard_map/while/body/eval_jaxpr/all_to_all | solution.py:95
  398.9 12.8 %all-to-all-done = bf16[32,4,1600]{2,1,0:T(4,128)(2,1)S(1)} async-done(((bf16[32,4,1600]{2,1,0:T(4,128)(2,1)}), bf16[32,4,1600]{2,1,0:T(4,128)(2,1)S(1)}, u32[]{:S(2)}, u32[]{:S(2)}) %all-to-all-start) | async-done | bytes 409632 | tf_op jit(solution)/shard_map/while/body/eval_jaxpr/all_to_all | solution.py:95
  435.4 12.8 %all-to-all-done = bf16[32,4,1600]{2,1,0:T(4,128)(2,1)S(1)} async-done(((bf16[32,4,1600]{2,1,0:T(4,128)(2,1)}), bf16[32,4,1600]{2,1,0:T(4,128)(2,1)S(1)}, u32[]{:S(2)}, u32[]{:S(2)}) %all-to-all-start) | async-done | bytes 409632 | tf_op jit(solution)/shard_map/while/body/eval_jaxpr/all_to_all | solution.py:95
  455.6 5.6 collective-permute-done
  472.0 12.8 %all-to-all-done = bf16[32,4,1600]{2,1,0:T(4,128)(2,1)S(1)} async-done(((bf16[32,4,1600]{2,1,0:T(4,128)(2,1)}), bf16[32,4,1600]{2,1,0:T(4,128)(2,1)S(1)}, u32[]{:S(2)}, u32[]{:S(2)}) %all-to-all-start) | async-done | bytes 409632 | tf_op jit(solution)/shard_map/while/body/eval_jaxpr/all_to_all | solution.py:95
  508.6 12.8 %all-to-all-done = bf16[32,4,1600]{2,1,0:T(4,128)(2,1)S(1)} async-done(((bf16[32,4,1600]{2,1,0:T(4,128)(2,1)}), bf16[32,4,1600]{2,1,0:T(4,128)(2,1)S(1)}, u32[]{:S(2)}, u32[]{:S(2)}) %all-to-all-start) | async-done | bytes 409632 | tf_op jit(solution)/shard_map/while/body/eval_jaxpr/all_to_all | solution.py:95
  545.2 12.8 %all-to-all-done = bf16[32,4,1600]{2,1,0:T(4,128)(2,1)S(1)} async-done(((bf16[32,4,1600]{2,1,0:T(4,128)(2,1)}), bf16[32,4,1600]{2,1,0:T(4,128)(2,1)S(1)}, u32[]{:S(2)}, u32[]{:S(2)}) %all-to-all-start) | async-done | bytes 409632 | tf_op jit(solution)/shard_map/while/body/eval_jaxpr/all_to_all | solution.py:95
  581.8 12.8 %all-to-all-done = bf16[32,4,1600]{2,1,0:T(4,128)(2,1)S(1)} async-done(((bf16[32,4,1600]{2,1,0:T(4,128)(2,1)}), bf16[32,4,1600]{2,1,0:T(4,128)(2,1)S(1)}, u32[]{:S(2)}, u32[]{:S(2)}) %all-to-all-start) | async-done | bytes 409632 | tf_op jit(solution)/shard_map/while/body/eval_jaxpr/all_to_all | solution.py:95
  618.4 12.8 %all-to-all-done = bf16[32,4,1600]{2,1,0:T(4,128)(2,1)S(1)} async-done(((bf16[32,4,1600]{2,1,0:T(4,128)(2,1)}), bf16[32,4,1600]{2,1,0:T(4,128)(2,1)S(1)}, u32[]{:S(2)}, u32[]{:S(2)}) %all-to-all-start) | async-done | bytes 409632 | tf_op jit(solution)/shard_map/while/body/eval_jaxpr/all_to_all | solution.py:95
  (396 shorter events, 371.0 us)
Async XLA Ops:
  5.8 27.0 %all-to-all-start.1 = ((s32[32,1,4]{2,1,0:T(1,128)}), s32[32,1,4]{2,1,0:T(1,128)S(1)}, u32[]{:S(2)}, u32[]{:S(2)}) async-start(s32[32,1,4]{2,1,0:T(1,128)} %bitcast.8), calls=%async_computation.1 | async-start | bytes 32768 | tf_op jit(solution)/shard_map/all_to_all | solution.py:77
  46.9 25.7 %all-to-all-start = ((bf16[32,4,1600]{2,1,0:T(4,128)(2,1)}), bf16[32,4,1600]{2,1,0:T(4,128)(2,1)S(1)}, u32[]{:S(2)}, u32[]{:S(2)}) async-start(bf16[32,4,1600]{2,1,0:T(4,128)(2,1)} %reshape.257), calls=%async_computation | async-start | bytes 851968 | tf_op jit(solution)/shard_map/while/body/eval_jaxpr/all_to_all | solution.py:95
  78.0 7.5 %collective-permute-start = (bf16[56,100,16]{1,2,0:T(8,128)(2,1)}, bf16[56,100,16]{1,2,0:T(8,128)(2,1)S(1)}, u32[]{:S(2)}, u32[]{:S(2)}) collective-permute-start(bf16[56,100,16]{1,2,0:T(8,128)(2,1)} %get-tuple-element.232), channel_id=1, source_target_pairs={{0,32},{32,64},{64,96},{96,128},{128,160},{160,192},{192,224},{224... | collective-permute-start | bytes 537608 | tf_op jit(solution)/shard_map/while/body/eval_jaxpr/ppermute | solution.py:16
  90.8 20.6 %all-to-all-start = ((bf16[32,4,1600]{2,1,0:T(4,128)(2,1)}), bf16[32,4,1600]{2,1,0:T(4,128)(2,1)S(1)}, u32[]{:S(2)}, u32[]{:S(2)}) async-start(bf16[32,4,1600]{2,1,0:T(4,128)(2,1)} %reshape.257), calls=%async_computation | async-start | bytes 851968 | tf_op jit(solution)/shard_map/while/body/eval_jaxpr/all_to_all | solution.py:95
  116.8 7.5 %collective-permute-start = (bf16[56,100,16]{1,2,0:T(8,128)(2,1)}, bf16[56,100,16]{1,2,0:T(8,128)(2,1)S(1)}, u32[]{:S(2)}, u32[]{:S(2)}) collective-permute-start(bf16[56,100,16]{1,2,0:T(8,128)(2,1)} %get-tuple-element.232), channel_id=1, source_target_pairs={{0,32},{32,64},{64,96},{96,128},{128,160},{160,192},{192,224},{224... | collective-permute-start | bytes 537608 | tf_op jit(solution)/shard_map/while/body/eval_jaxpr/ppermute | solution.py:16
  129.5 21.4 %all-to-all-start = ((bf16[32,4,1600]{2,1,0:T(4,128)(2,1)}), bf16[32,4,1600]{2,1,0:T(4,128)(2,1)S(1)}, u32[]{:S(2)}, u32[]{:S(2)}) async-start(bf16[32,4,1600]{2,1,0:T(4,128)(2,1)} %reshape.257), calls=%async_computation | async-start | bytes 851968 | tf_op jit(solution)/shard_map/while/body/eval_jaxpr/all_to_all | solution.py:95
  156.4 7.5 %collective-permute-start = (bf16[56,100,16]{1,2,0:T(8,128)(2,1)}, bf16[56,100,16]{1,2,0:T(8,128)(2,1)S(1)}, u32[]{:S(2)}, u32[]{:S(2)}) collective-permute-start(bf16[56,100,16]{1,2,0:T(8,128)(2,1)} %get-tuple-element.232), channel_id=1, source_target_pairs={{0,32},{32,64},{64,96},{96,128},{128,160},{160,192},{192,224},{224... | collective-permute-start | bytes 537608 | tf_op jit(solution)/shard_map/while/body/eval_jaxpr/ppermute | solution.py:16
  169.1 20.2 %all-to-all-start = ((bf16[32,4,1600]{2,1,0:T(4,128)(2,1)}), bf16[32,4,1600]{2,1,0:T(4,128)(2,1)S(1)}, u32[]{:S(2)}, u32[]{:S(2)}) async-start(bf16[32,4,1600]{2,1,0:T(4,128)(2,1)} %reshape.257), calls=%async_computation | async-start | bytes 851968 | tf_op jit(solution)/shard_map/while/body/eval_jaxpr/all_to_all | solution.py:95
  207.5 19.8 %all-to-all-start = ((bf16[32,4,1600]{2,1,0:T(4,128)(2,1)}), bf16[32,4,1600]{2,1,0:T(4,128)(2,1)S(1)}, u32[]{:S(2)}, u32[]{:S(2)}) async-start(bf16[32,4,1600]{2,1,0:T(4,128)(2,1)} %reshape.257), calls=%async_computation | async-start | bytes 851968 | tf_op jit(solution)/shard_map/while/body/eval_jaxpr/all_to_all | solution.py:95
  245.4 19.7 %all-to-all-start = ((bf16[32,4,1600]{2,1,0:T(4,128)(2,1)}), bf16[32,4,1600]{2,1,0:T(4,128)(2,1)S(1)}, u32[]{:S(2)}, u32[]{:S(2)}) async-start(bf16[32,4,1600]{2,1,0:T(4,128)(2,1)} %reshape.257), calls=%async_computation | async-start | bytes 851968 | tf_op jit(solution)/shard_map/while/body/eval_jaxpr/all_to_all | solution.py:95
  270.6 7.5 %collective-permute-start = (bf16[56,100,16]{1,2,0:T(8,128)(2,1)}, bf16[56,100,16]{1,2,0:T(8,128)(2,1)S(1)}, u32[]{:S(2)}, u32[]{:S(2)}) collective-permute-start(bf16[56,100,16]{1,2,0:T(8,128)(2,1)} %get-tuple-element.232), channel_id=1, source_target_pairs={{0,32},{32,64},{64,96},{96,128},{128,160},{160,192},{192,224},{224... | collective-permute-start | bytes 537608 | tf_op jit(solution)/shard_map/while/body/eval_jaxpr/ppermute | solution.py:16
  283.3 18.6 %all-to-all-start = ((bf16[32,4,1600]{2,1,0:T(4,128)(2,1)}), bf16[32,4,1600]{2,1,0:T(4,128)(2,1)S(1)}, u32[]{:S(2)}, u32[]{:S(2)}) async-start(bf16[32,4,1600]{2,1,0:T(4,128)(2,1)} %reshape.257), calls=%async_computation | async-start | bytes 851968 | tf_op jit(solution)/shard_map/while/body/eval_jaxpr/all_to_all | solution.py:95
  307.3 7.5 %collective-permute-start = (bf16[56,100,16]{1,2,0:T(8,128)(2,1)}, bf16[56,100,16]{1,2,0:T(8,128)(2,1)S(1)}, u32[]{:S(2)}, u32[]{:S(2)}) collective-permute-start(bf16[56,100,16]{1,2,0:T(8,128)(2,1)} %get-tuple-element.232), channel_id=1, source_target_pairs={{0,32},{32,64},{64,96},{96,128},{128,160},{160,192},{192,224},{224... | collective-permute-start | bytes 537608 | tf_op jit(solution)/shard_map/while/body/eval_jaxpr/ppermute | solution.py:16
  320.1 18.4 %all-to-all-start = ((bf16[32,4,1600]{2,1,0:T(4,128)(2,1)}), bf16[32,4,1600]{2,1,0:T(4,128)(2,1)S(1)}, u32[]{:S(2)}, u32[]{:S(2)}) async-start(bf16[32,4,1600]{2,1,0:T(4,128)(2,1)} %reshape.257), calls=%async_computation | async-start | bytes 851968 | tf_op jit(solution)/shard_map/while/body/eval_jaxpr/all_to_all | solution.py:95
  343.9 7.5 %collective-permute-start = (bf16[56,100,16]{1,2,0:T(8,128)(2,1)}, bf16[56,100,16]{1,2,0:T(8,128)(2,1)S(1)}, u32[]{:S(2)}, u32[]{:S(2)}) collective-permute-start(bf16[56,100,16]{1,2,0:T(8,128)(2,1)} %get-tuple-element.232), channel_id=1, source_target_pairs={{0,32},{32,64},{64,96},{96,128},{128,160},{160,192},{192,224},{224... | collective-permute-start | bytes 537608 | tf_op jit(solution)/shard_map/while/body/eval_jaxpr/ppermute | solution.py:16
  356.6 18.4 %all-to-all-start = ((bf16[32,4,1600]{2,1,0:T(4,128)(2,1)}), bf16[32,4,1600]{2,1,0:T(4,128)(2,1)S(1)}, u32[]{:S(2)}, u32[]{:S(2)}) async-start(bf16[32,4,1600]{2,1,0:T(4,128)(2,1)} %reshape.257), calls=%async_computation | async-start | bytes 851968 | tf_op jit(solution)/shard_map/while/body/eval_jaxpr/all_to_all | solution.py:95
  393.2 18.4 %all-to-all-start = ((bf16[32,4,1600]{2,1,0:T(4,128)(2,1)}), bf16[32,4,1600]{2,1,0:T(4,128)(2,1)S(1)}, u32[]{:S(2)}, u32[]{:S(2)}) async-start(bf16[32,4,1600]{2,1,0:T(4,128)(2,1)} %reshape.257), calls=%async_computation | async-start | bytes 851968 | tf_op jit(solution)/shard_map/while/body/eval_jaxpr/all_to_all | solution.py:95
  417.0 7.5 %collective-permute-start = (bf16[56,100,16]{1,2,0:T(8,128)(2,1)}, bf16[56,100,16]{1,2,0:T(8,128)(2,1)S(1)}, u32[]{:S(2)}, u32[]{:S(2)}) collective-permute-start(bf16[56,100,16]{1,2,0:T(8,128)(2,1)} %get-tuple-element.232), channel_id=1, source_target_pairs={{0,32},{32,64},{64,96},{96,128},{128,160},{160,192},{192,224},{224... | collective-permute-start | bytes 537608 | tf_op jit(solution)/shard_map/while/body/eval_jaxpr/ppermute | solution.py:16
  429.8 18.4 %all-to-all-start = ((bf16[32,4,1600]{2,1,0:T(4,128)(2,1)}), bf16[32,4,1600]{2,1,0:T(4,128)(2,1)S(1)}, u32[]{:S(2)}, u32[]{:S(2)}) async-start(bf16[32,4,1600]{2,1,0:T(4,128)(2,1)} %reshape.257), calls=%async_computation | async-start | bytes 851968 | tf_op jit(solution)/shard_map/while/body/eval_jaxpr/all_to_all | solution.py:95
  466.4 18.4 %all-to-all-start = ((bf16[32,4,1600]{2,1,0:T(4,128)(2,1)}), bf16[32,4,1600]{2,1,0:T(4,128)(2,1)S(1)}, u32[]{:S(2)}, u32[]{:S(2)}) async-start(bf16[32,4,1600]{2,1,0:T(4,128)(2,1)} %reshape.257), calls=%async_computation | async-start | bytes 851968 | tf_op jit(solution)/shard_map/while/body/eval_jaxpr/all_to_all | solution.py:95
  503.0 18.4 %all-to-all-start = ((bf16[32,4,1600]{2,1,0:T(4,128)(2,1)}), bf16[32,4,1600]{2,1,0:T(4,128)(2,1)S(1)}, u32[]{:S(2)}, u32[]{:S(2)}) async-start(bf16[32,4,1600]{2,1,0:T(4,128)(2,1)} %reshape.257), calls=%async_computation | async-start | bytes 851968 | tf_op jit(solution)/shard_map/while/body/eval_jaxpr/all_to_all | solution.py:95
  539.5 18.4 %all-to-all-start = ((bf16[32,4,1600]{2,1,0:T(4,128)(2,1)}), bf16[32,4,1600]{2,1,0:T(4,128)(2,1)S(1)}, u32[]{:S(2)}, u32[]{:S(2)}) async-start(bf16[32,4,1600]{2,1,0:T(4,128)(2,1)} %reshape.257), calls=%async_computation | async-start | bytes 851968 | tf_op jit(solution)/shard_map/while/body/eval_jaxpr/all_to_all | solution.py:95
  576.1 18.4 %all-to-all-start = ((bf16[32,4,1600]{2,1,0:T(4,128)(2,1)}), bf16[32,4,1600]{2,1,0:T(4,128)(2,1)S(1)}, u32[]{:S(2)}, u32[]{:S(2)}) async-start(bf16[32,4,1600]{2,1,0:T(4,128)(2,1)} %reshape.257), calls=%async_computation | async-start | bytes 851968 | tf_op jit(solution)/shard_map/while/body/eval_jaxpr/all_to_all | solution.py:95
  612.7 18.4 %all-to-all-start = ((bf16[32,4,1600]{2,1,0:T(4,128)(2,1)}), bf16[32,4,1600]{2,1,0:T(4,128)(2,1)S(1)}, u32[]{:S(2)}, u32[]{:S(2)}) async-start(bf16[32,4,1600]{2,1,0:T(4,128)(2,1)} %reshape.257), calls=%async_computation | async-start | bytes 851968 | tf_op jit(solution)/shard_map/while/body/eval_jaxpr/all_to_all | solution.py:95
  (28 other events, 100.3 us)
where the time goes:
time: 642 us; the launch traced here: 639 us
  waiting for transfers between devices  305 us (48%)
  starting transfers between devices  122 us (19%)
  matrix products  103 us (16%)
  local copies, waits for them, and re-layouts  102 us (16%)
    all_to_all x16, waiting for transfers between devices, section_turn(): lax.all_to_all(outbox.reshape(span_count, width, U * R), 'span', split_ax...  216 us
    ppermute x16, waiting for transfers between devices, passed_along(): lax.ppermute(value, axis, [(source, source + steps) for source in range(l...  89.5 us
    all_to_all x16, starting transfers between devices, section_turn(): lax.all_to_all(outbox.reshape(span_count, width, U * R), 'span', split_ax...  81 us
    dot_general x16, matrix products, apply_inverse(): jnp.einsum('nij,njr->nir', inverse_blocks, merged, preferred_element_type...  67 us
    dot_general x16, matrix products, piece_terms(): jnp.einsum('nij,njr->nir', face_blocks, nearby, preferred_element_type=jn...  33.1 us
    ppermute x16, starting transfers between devices, passed_along(): lax.ppermute(value, axis, [(source, source + steps) for source in range(l...  30.5 us
    scatter x16, local copies, waits for them, and re-layouts, section_turn(): outbox = jnp.zeros((span_count * width, U * R), jnp.bfloat16).at[position...  15.9 us
    reshape x16, local copies, waits for them, and re-layouts, section_turn(): outbox.reshape(span_count, width, U * R)  13.7 us
  transfers between devices with their start and end apart: 33, of which 32 were waited for; matrix products, arithmetic and copies ran while one was open for 5% of the time, Pallas kernels for 0%

commit v1 on v0

v1 whole, which is shorter than its diff:
```python
import functools

import jax
import jax.numpy as jnp
from jax import lax
from jax.experimental import pallas as pl
from jax.experimental.pallas import tpu as pltpu
from jax.sharding import PartitionSpec as P

U = 100
R = 16
LANES = 128
GROUPS = 2
CAP = 2
MSG = CAP * R
BLOCK = 4
MESH = pl.DeviceIdType.MESH


def times_transposed(states, block):
    return lax.dot_general(
        states, block, (((1,), (1,)), ((), ())), preferred_element_type=jnp.float32
    )


def section_kernel(
    sizes,
    up_cells,
    piece_up,
    owner_row,
    cell_row,
    right_side,
    piece_rhs,
    up_blocks,
    inverses,
    piece_blocks,
    out,
    face_pad,
    inverse_pad,
    piece_pad,
    rhs_pad,
    piece_rhs_pad,
    table,
    slot_table,
    index_out,
    index_in,
    selector,
    outbox,
    inbox,
    arrived_0,
    arrived_1,
    sent,
    owned,
    table_sem,
    index_sems,
    outbox_sems,
    inbox_sems,
    sent_sems,
    arrived_sems,
):
    sections, span_x, span_y, cells, slots = sizes
    span = span_x * span_y
    cell_grp, slot_grp = cells // GROUPS, slots // GROUPS
    section = lax.axis_index("stream")
    me = lax.axis_index("span")
    me_x, me_y = me // span_y, me % span_y

    def peer(turn):
        x = (me_x + turn // span_y) % span_x
        y = (me_y + turn % span_y) % span_y
        return x * span_y + y

    arrived = (arrived_0, arrived_1)
    barrier = pltpu.get_barrier_semaphore()

    @pl.loop(1, span)
    def _(turn):
        pl.semaphore_signal(barrier, inc=1, device_id={"span": peer(turn)}, device_id_type=MESH)

    for step in (1, sections - 1):
        pl.semaphore_signal(
            barrier, inc=1, device_id={"stream": (section + step) % sections}, device_id_type=MESH
        )

    turn_col = lax.broadcasted_iota(jnp.int32, (span, slots), 0)
    slot_lane = lax.broadcasted_iota(jnp.int32, (span, slots), 1)
    match = owner_row[...] == peer(turn_col)
    lane = lax.broadcasted_iota(jnp.int32, (span, LANES), 1)
    mine = lane // MSG == lax.broadcasted_iota(jnp.int32, (span, LANES), 0) % BLOCK
    slot_values = jnp.zeros((span, LANES), jnp.int32)
    for group in range(GROUPS):
        indices = jnp.zeros((span, LANES), jnp.int32)
        named = match & (slot_lane // slot_grp == group)
        lowest = jnp.min(jnp.where(named, slot_lane, slots), axis=1, keepdims=True)
        highest = jnp.max(jnp.where(named, slot_lane, -1), axis=1, keepdims=True)
        found = (highest >= lowest, highest > lowest)
        for place, piece in enumerate((lowest, highest)):
            chosen = (slot_lane == piece) & found[place]
            piece = jnp.where(found[place], piece, group * slot_grp)
            target = jnp.sum(jnp.where(chosen, cell_row[...] + 1, 0), axis=1, keepdims=True)
            slot_values = jnp.where(
                lane == group * CAP + place, piece, slot_values
            )
            indices = jnp.where(mine & (lane // R % CAP == place), target, indices)
        index_out[:, group, :] = indices
    table[...] = slot_values
    to_slots = pltpu.make_async_copy(table, slot_table, table_sem)
    to_slots.start()

    def padded(source, target, count):
        target[...] = jnp.zeros_like(target)

        @pl.loop(0, count)
        def _(i):
            target[i, : source.shape[1], : source.shape[2]] = source[i]

    padded(right_side, rhs_pad, cells)
    padded(piece_rhs, piece_rhs_pad, slots)

    to_slots.wait()
    pl.semaphore_wait(barrier, span + 1)

    index_in[0] = index_out[0]

    @pl.loop(1, span)
    def _(turn):
        pltpu.make_async_remote_copy(
            src_ref=index_out.at[turn],
            dst_ref=index_in.at[turn],
            send_sem=index_sems.at[0],
            recv_sem=index_sems.at[1],
            device_id={"span": peer(turn)},
            device_id_type=MESH,
        ).start()

    padded(piece_blocks, piece_pad, slots)
    padded(up_blocks, face_pad, 2 * cells)
    padded(inverses, inverse_pad, cells)

    remote = pl.ds(1, span - 1)
    pltpu.make_async_copy(index_in.at[remote], index_in.at[remote], index_sems.at[1]).wait()
    row = lax.broadcasted_iota(jnp.int32, (cell_grp * R, LANES), 0)
    column = lax.broadcasted_iota(jnp.int32, (cell_grp * R, LANES), 1)
    same_side = row % R == column % R
    for group in range(GROUPS):
        for part in range(span // BLOCK):
            named = index_in[BLOCK * part, pl.ds(group, 1), :]
            for j in range(1, BLOCK):
                named = named + index_in[BLOCK * part + j, pl.ds(group, 1), :]
            hit = same_side & (row // R + 1 == named)
            selector[group, :, pl.ds(part * LANES, LANES)] = hit.astype(jnp.bfloat16)

    def start_group(group):
        @pl.when(section == 0)
        def _():
            arrived[group][...] = jnp.zeros_like(arrived[group])

        @pl.when(section > 0)
        def _():
            pltpu.make_async_copy(
                arrived[group], arrived[group], arrived_sems.at[group]
            ).wait()

        def part(index, own_first):
            for j in range(BLOCK):
                turn = index * BLOCK + j
                for place in range(CAP):
                    piece = slot_table[turn, group * CAP + place]
                    near = arrived[group][piece_up[piece]]
                    term = piece_rhs_pad[piece].astype(jnp.float32) - times_transposed(
                        near, piece_pad[piece]
                    )
                    term = term.astype(jnp.bfloat16)
                    if own_first and j == 0:
                        inbox[group, 0, pl.ds(place * R, R), :] = term
                    else:
                        outbox[group, turn, pl.ds(place * R, R), :] = term
            for j in range(1 if own_first else 0, BLOCK):
                turn = index * BLOCK + j
                pltpu.make_async_remote_copy(
                    src_ref=outbox.at[group, turn],
                    dst_ref=inbox.at[group, turn],
                    send_sem=outbox_sems.at[group],
                    recv_sem=inbox_sems.at[group],
                    device_id={"span": peer(turn)},
                    device_id_type=MESH,
                ).start()

        @pl.loop(1, span // BLOCK)
        def _(index):
            part(index, False)

        part(0, True)

        @pl.loop(0, cell_grp // BLOCK)
        def _(index):
            for j in range(BLOCK):
                cell = index * BLOCK + j
                whole = group * cell_grp + cell
                total = rhs_pad[whole].astype(jnp.float32)
                for face in range(2):
                    near = arrived[group][up_cells[whole, face]]
                    total = total - times_transposed(near, face_pad[2 * whole + face])
                owned[group, cell] = total

    def finish_group(group):
        pltpu.make_async_copy(
            inbox.at[group, remote], inbox.at[group, remote], inbox_sems.at[group]
        ).wait()
        messages = inbox[group].reshape(span * MSG, LANES)
        summed = jnp.dot(selector[group], messages, preferred_element_type=jnp.float32)
        owned[group] = owned[group] + summed.reshape(cell_grp, R, LANES)

        @pl.loop(0, cell_grp // BLOCK)
        def _(index):
            for j in range(BLOCK):
                cell = index * BLOCK + j
                whole = group * cell_grp + cell
                merged = owned[group, cell].astype(jnp.bfloat16)
                sent[group, cell] = times_transposed(merged, inverse_pad[whole]).astype(
                    jnp.bfloat16
                )

        @pl.when(section < sections - 1)
        def _():
            downstream(group).start()

        out[pl.ds(group * cell_grp, cell_grp)] = sent[group, :, :, :U]

    def downstream(group):
        return pltpu.make_async_remote_copy(
            src_ref=sent.at[group],
            dst_ref=arrived[group],
            send_sem=sent_sems.at[group],
            recv_sem=arrived_sems.at[group],
            device_id={"stream": (section + 1) % sections},
            device_id_type=MESH,
        )

    for group in range(GROUPS):
        start_group(group)
    for group in range(GROUPS):
        finish_group(group)

    pltpu.make_async_copy(index_out.at[remote], index_out.at[remote], index_sems.at[0]).wait()
    for group in range(GROUPS):
        pltpu.make_async_copy(
            outbox.at[group, remote], outbox.at[group, remote], outbox_sems.at[group]
        ).wait()

        @pl.when(section < sections - 1)
        def _():
            downstream(group).wait_send()


def on_device(
    sizes,
    right_side,
    up_blocks,
    inverses,
    up_cells,
    piece_rhs,
    piece_blocks,
    piece_up,
    piece_owner,
    piece_cell,
):
    sections, span_x, span_y, cells, slots = sizes
    span = span_x * span_y
    cell_grp = cells // GROUPS
    vmem = pl.BlockSpec(memory_space=pltpu.VMEM)
    smem = pl.BlockSpec(memory_space=pltpu.SMEM)
    bf16 = jnp.bfloat16
    states = pl.pallas_call(
        functools.partial(section_kernel, sizes),
        out_shape=jax.ShapeDtypeStruct((cells, R, U), bf16),
        in_specs=[smem, smem] + [vmem] * 7,
        out_specs=vmem,
        scratch_shapes=[
            pltpu.VMEM((2 * cells, LANES, LANES), bf16),
            pltpu.VMEM((cells, LANES, LANES), bf16),
            pltpu.VMEM((slots, LANES, LANES), bf16),
            pltpu.VMEM((cells, R, LANES), bf16),
            pltpu.VMEM((slots, R, LANES), bf16),
            pltpu.VMEM((span, LANES), jnp.int32),
            pltpu.SMEM((span, LANES), jnp.int32),
            pltpu.VMEM((span, GROUPS, LANES), jnp.int32),
            pltpu.VMEM((span, GROUPS, LANES), jnp.int32),
            pltpu.VMEM((GROUPS, cell_grp * R, span * MSG), bf16),
            pltpu.VMEM((GROUPS, span, MSG, LANES), bf16),
            pltpu.VMEM((GROUPS, span, MSG, LANES), bf16),
            pltpu.VMEM((cell_grp, R, LANES), bf16),
            pltpu.VMEM((cell_grp, R, LANES), bf16),
            pltpu.VMEM((GROUPS, cell_grp, R, LANES), bf16),
            pltpu.VMEM((GROUPS, cell_grp, R, LANES), jnp.float32),
            pltpu.SemaphoreType.DMA,
            pltpu.SemaphoreType.DMA((2,)),
            pltpu.SemaphoreType.DMA((GROUPS,)),
            pltpu.SemaphoreType.DMA((GROUPS,)),
            pltpu.SemaphoreType.DMA((GROUPS,)),
            pltpu.SemaphoreType.DMA((GROUPS,)),
        ],
        compiler_params=pltpu.CompilerParams(
            collective_id=0, has_side_effects=True, vmem_limit_bytes=48 * 1024 * 1024
        ),
    )(
        up_cells[0],
        piece_up[0],
        piece_owner.reshape(1, slots),
        piece_cell.reshape(1, slots),
        right_side.reshape(cells, U, R).swapaxes(1, 2),
        piece_rhs.reshape(slots, U, R).swapaxes(1, 2),
        up_blocks.reshape(2 * cells, U, U),
        inverses.reshape(cells, U, U),
        piece_blocks.reshape(slots, U, U),
    )
    return states.swapaxes(1, 2).reshape(1, cells, U * R)


def solution(mesh):
    sections, span = mesh.shape["stream"], mesh.shape["span"]
    span_x = 4 if span == 32 else 2
    sizes = (sections, span_x, span // span_x, 56, 48)
    in_specs = (
        P("stream", "span", None),
        P("stream", "span", None),
        P("stream", "span", None),
        P("stream", "span", None),
        P("stream", "span", None),
        P("stream", "span", None),
        P("stream", "span"),
        P("stream", "span", None),
        P("stream", "span"),
    )
    out_specs = P("stream", "span", None)
    return jax.shard_map(
        functools.partial(on_device, sizes),
        mesh=mesh,
        in_specs=in_specs,
        out_specs=out_specs,
        check_vma=False,
    )
```

time: 642 us -> 223 us (0.35)
  the two profiles are of different devices: /device:TPU:72 before, /device:TPU:449 now
where the time goes in v1:
time: 223 us; the launch traced here: 222 us
  Pallas kernels  204 us (91%)
  local copies, waits for them, and re-layouts  18.1 us (8%)
    pallas_call x1, Pallas kernels, on_device(): pl.pallas_call(functools.partial(section_kernel, sizes), out_shape=jax.Sh...  204 us
    reshape x1, local copies, waits for them, and re-layouts, on_device(): up_blocks.reshape(2 * cells, U, U)  7.81 us

profile of v1, /device:TPU:449, one launch (start us, length us, event | category | flops | bytes accessed | tf_op | source)
XLA Modules:
  0.0 222.3 jit_solution(15797124961768203476)
XLA Ops:
  0.0 0.0 copy-start.3
  0.0 0.8 copy.15.up_cells
  0.9 1.2 copy.11
  2.0 0.5 copy.12
  2.5 1.2 copy.13
  3.7 0.5 copy.14
  4.2 0.0 copy-done.3
  4.2 1.6 reshape.26.piece_blocks
  5.9 3.1 %reshape.25.inverses = bf16[56,100,100]{2,1,0:T(8,128)(2,1)S(1)} reshape(bf16[1,56,10000]{2,1,0:T(8,128)(2,1)} %param.11) | data formatting | bytes 2240000 | tf_op jit(solution)/shard_map/reshape | solution.py:314
  9.0 0.0 copy-start
  9.0 0.0 copy-start.1
  9.0 0.0 copy-start.2
  9.0 7.8 %reshape.24.up_blocks = bf16[112,100,100]{2,1,0:T(8,128)(2,1)} reshape(bf16[1,56,20000]{2,1,0:T(8,128)(2,1)} %param.10) | data formatting | bytes 4480000 | tf_op jit(solution)/shard_map/reshape | solution.py:313
  16.8 0.0 copy-done
  16.8 0.0 copy-done.1
  16.8 0.0 copy-done.2
  16.8 204.1 %shard_map.91 = bf16[56,16,100]{2,1,0:T(8,128)(2,1)S(1)} custom-call(s32[56,2]{1,0:T(8,128)S(1)} %copy.15.up_cells, s32[48]{0:T(128)S(1)} %bitcast.12, s32[1,48]{1,0:T(1,128)S(1)} %bitcast.13, s32[1,48]{1,0:T(1,128)S(1)} %copy-done.2, bf16[56,16,100]{2,1,0:T(8,128)(2,1)S(1)} %bitcast.9, bf16[48,16,100]{2,1,0:T(8,128)(2,1)S(1)} %bitcast.11, ...), custom_call_target="tpu_custom_call" | custom-call | tf_op jit(solution)/shard_map/pallas_call | solution.py:274
  220.9 0.5 copy.16
  221.4 0.9 copy.17
Async XLA Ops:
  0.0 4.2 %copy-start.3 = (bf16[1,48,10000]{2,1,0:T(8,128)(2,1)S(1)}, bf16[1,48,10000]{2,1,0:T(8,128)(2,1)}, u32[]{:S(2)}) copy-start(bf16[1,48,10000]{2,1,0:T(8,128)(2,1)} %param.14) | copy-start | bytes 2880004
  9.0 7.8 %copy-start = (s32[1,48]{1,0:T(1,128)S(1)}, s32[1,48]{1,0:T(1,128)}, u32[]{:S(2)}) copy-start(s32[1,48]{1,0:T(1,128)} %param.15) | copy-start | bytes 580
  9.0 7.8 %copy-start.1 = (s32[1,48,1]{1,2,0:T(1,128)S(1)}, s32[1,48,1]{1,2,0:T(1,128)}, u32[]{:S(2)}) copy-start(s32[1,48,1]{1,2,0:T(1,128)} %param.16) | copy-start | bytes 580
  9.0 7.8 %copy-start.2 = (s32[1,48]{1,0:T(1,128)S(1)}, s32[1,48]{1,0:T(1,128)}, u32[]{:S(2)}) copy-start(s32[1,48]{1,0:T(1,128)} %cell_row.1) | copy-start | bytes 580

commit v2 on v1

v2 whole, which is shorter than its diff:
```python
import functools

import jax
import jax.numpy as jnp
from jax import lax
from jax.experimental import pallas as pl
from jax.experimental.pallas import tpu as pltpu
from jax.sharding import PartitionSpec as P

U = 100
R = 16
LANES = 128
GROUPS = 2
CAP = 2
MSG = CAP * R
BLOCK = 4
HALF = 14
UP_LANE = 64
MESH = pl.DeviceIdType.MESH


def times_transposed(states, block):
    return lax.dot_general(
        states, block, (((1,), (1,)), ((), ())), preferred_element_type=jnp.float32
    )


def section_kernel(
    sizes,
    up_cells,
    owner_row,
    cell_row,
    up_row,
    right_side,
    piece_rhs,
    up_blocks,
    inverses,
    piece_blocks,
    out,
    face_t,
    inverse_t,
    piece_pad,
    rhs_pad,
    piece_rhs_pad,
    next_piece,
    next_rhs,
    coupling,
    table,
    next_table,
    own_slots,
    slots_next,
    index_out,
    index_in,
    selector,
    first_box,
    outbox,
    inbox,
    arrived_0,
    arrived_1,
    sent,
    owned,
    merged,
    table_sems,
    ship_sems,
    ship_recv_sems,
    index_sems,
    first_sems,
    outbox_sems,
    inbox_sems,
    sent_sems,
    arrived_sems,
):
    sections, span_x, span_y, cells, slots = sizes
    span = span_x * span_y
    cell_grp, slot_grp = cells // GROUPS, slots // GROUPS
    section = lax.axis_index("stream")
    me = lax.axis_index("span")
    me_x, me_y = me // span_y, me % span_y
    after, ahead = (section + 1) % sections, (section + sections - 1) % sections
    arrived = (arrived_0, arrived_1)
    remote = pl.ds(1, span - 1)
    is_first, is_last = section == 0, section == sections - 1

    def peer(turn):
        x = (me_x + turn // span_y) % span_x
        y = (me_y + turn % span_y) % span_y
        return x * span_y + y

    def whole_wait(ref, sem):
        pltpu.make_async_copy(ref, ref, sem).wait()

    barrier = pltpu.get_barrier_semaphore()

    @pl.loop(0, span)
    def _(turn):
        pl.semaphore_signal(
            barrier,
            inc=1,
            device_id={"stream": ahead, "span": peer(turn)},
            device_id_type=MESH,
        )

    @pl.loop(1, span)
    def _(turn):
        pl.semaphore_signal(barrier, inc=1, device_id={"span": peer(turn)}, device_id_type=MESH)

    pl.semaphore_signal(barrier, inc=1, device_id={"stream": after}, device_id_type=MESH)

    turn_col = lax.broadcasted_iota(jnp.int32, (span, slots), 0)
    slot_lane = lax.broadcasted_iota(jnp.int32, (span, slots), 1)
    match = owner_row[...] == peer(turn_col)
    lane = lax.broadcasted_iota(jnp.int32, (span, LANES), 1)
    mine = lane // MSG == lax.broadcasted_iota(jnp.int32, (span, LANES), 0) % BLOCK
    slot_values = jnp.zeros((span, LANES), jnp.int32)
    for group in range(GROUPS):
        indices = jnp.zeros((span, LANES), jnp.int32)
        named = match & (slot_lane // slot_grp == group)
        lowest = jnp.min(jnp.where(named, slot_lane, slots), axis=1, keepdims=True)
        highest = jnp.max(jnp.where(named, slot_lane, -1), axis=1, keepdims=True)
        found = (highest >= lowest, highest > lowest)
        for place, piece in enumerate((lowest, highest)):
            chosen = (slot_lane == piece) & found[place]
            piece = jnp.where(found[place], piece, group * slot_grp)
            target = jnp.sum(jnp.where(chosen, cell_row[...] + 1, 0), axis=1, keepdims=True)
            source = jnp.sum(jnp.where(chosen, up_row[...], 0), axis=1, keepdims=True)
            column = group * CAP + place
            slot_values = jnp.where(lane == column, piece, slot_values)
            slot_values = jnp.where(lane == GROUPS * CAP + column, source, slot_values)
            indices = jnp.where(mine & (lane // R % CAP == place), target, indices)
        index_out[:, group, :] = indices
    table[...] = slot_values
    table[:, UP_LANE : UP_LANE + slots] = jnp.broadcast_to(up_row[...], (span, slots))

    @pl.when(is_first)
    def _():
        pltpu.make_async_copy(table, own_slots, table_sems.at[0]).start()

    def padded(source, target, count):
        target[...] = jnp.zeros_like(target)

        @pl.loop(0, count)
        def _(i):
            target[i, : source.shape[1], : source.shape[2]] = source[i]

    def transposed(target, count):
        @pl.loop(0, count // BLOCK)
        def _(index):
            for j in range(BLOCK):
                i = index * BLOCK + j
                target[i] = target[i].astype(jnp.float32).T.astype(jnp.bfloat16)

    padded(piece_rhs, piece_rhs_pad, slots)
    padded(piece_blocks, piece_pad, slots)
    padded(right_side, rhs_pad, cells)

    pl.semaphore_wait(barrier, 2 * span)

    def shipments():
        return [
            pltpu.make_async_remote_copy(
                src_ref=source,
                dst_ref=target,
                send_sem=ship_sems.at[i],
                recv_sem=ship_recv_sems.at[i],
                device_id={"stream": ahead},
                device_id_type=MESH,
            )
            for i, (source, target) in enumerate(
                ((table, next_table), (piece_rhs_pad, next_rhs), (piece_pad, next_piece))
            )
        ]

    @pl.when(section > 0)
    def _():
        for copy in shipments():
            copy.start()

    index_in[0] = index_out[0]

    @pl.loop(1, span)
    def _(turn):
        pltpu.make_async_remote_copy(
            src_ref=index_out.at[turn],
            dst_ref=index_in.at[turn],
            send_sem=index_sems.at[0],
            recv_sem=index_sems.at[1],
            device_id={"span": peer(turn)},
            device_id_type=MESH,
        ).start()

    @pl.when(is_first)
    def _():
        pltpu.make_async_copy(table, own_slots, table_sems.at[0]).wait()
        for group in range(GROUPS):
            for place in range(CAP):
                piece = own_slots[0, group * CAP + place]
                inbox[group, 0, pl.ds(place * R, R), :] = piece_rhs_pad[piece]

            @pl.loop(1, span)
            def _(turn):
                for place in range(CAP):
                    piece = own_slots[turn, group * CAP + place]
                    first_box[group, turn, pl.ds(place * R, R), :] = piece_rhs_pad[piece]
                pltpu.make_async_remote_copy(
                    src_ref=first_box.at[group, turn],
                    dst_ref=inbox.at[group, turn],
                    send_sem=first_sems.at[group],
                    recv_sem=inbox_sems.at[group],
                    device_id={"span": peer(turn)},
                    device_id_type=MESH,
                ).start()

    padded(inverses, inverse_t, cells)
    transposed(inverse_t, cells)

    @pl.when(jnp.logical_not(is_last))
    def _():
        whole_wait(next_table, ship_recv_sems.at[0])
        to_slots = pltpu.make_async_copy(next_table, slots_next, table_sems.at[1])
        to_slots.start()
        whole_wait(next_rhs, ship_recv_sems.at[1])
        whole_wait(next_piece, ship_recv_sems.at[2])
        to_slots.wait()
        for group in range(GROUPS):

            @pl.loop(0, slot_grp // BLOCK)
            def _(index):
                for j in range(BLOCK):
                    piece = group * slot_grp + index * BLOCK + j
                    cell = group * cell_grp + slots_next[0, UP_LANE + piece]
                    coupling[piece] = times_transposed(inverse_t[cell], next_piece[piece]).astype(
                        jnp.bfloat16
                    )

    @pl.when(section > 0)
    def _():
        padded(up_blocks, face_t, 2 * cells)
        transposed(face_t, 2 * cells)

    whole_wait(index_in.at[remote], index_sems.at[1])
    row = lax.broadcasted_iota(jnp.int32, (cell_grp * R, LANES), 0)
    column = lax.broadcasted_iota(jnp.int32, (cell_grp * R, LANES), 1)
    same_side = row % R == column % R
    for group in range(GROUPS):
        for part in range(span // BLOCK):
            named = index_in[BLOCK * part, pl.ds(group, 1), :]
            for j in range(1, BLOCK):
                named = named + index_in[BLOCK * part + j, pl.ds(group, 1), :]
            hit = same_side & (row // R + 1 == named)
            selector[group, :, pl.ds(part * LANES, LANES)] = hit.astype(jnp.bfloat16)

    def downstream(group, half):
        cells_of = pl.ds(half * HALF, HALF)
        return pltpu.make_async_remote_copy(
            src_ref=sent.at[group, cells_of],
            dst_ref=arrived[group].at[cells_of],
            send_sem=sent_sems.at[group],
            recv_sem=arrived_sems.at[group],
            device_id={"stream": after},
            device_id_type=MESH,
        )

    def own_terms(group):
        @pl.when(is_first)
        def _():
            owned[group] = rhs_pad[pl.ds(group * cell_grp, cell_grp)].astype(jnp.float32)

        @pl.when(section > 0)
        def _():
            whole_wait(arrived[group], arrived_sems.at[group])

            @pl.loop(0, cell_grp // 7)
            def _(index):
                for j in range(7):
                    cell = index * 7 + j
                    whole = group * cell_grp + cell
                    total = rhs_pad[whole].astype(jnp.float32)
                    for face in range(2):
                        near = arrived[group][up_cells[whole, face]]
                        total = total - jnp.dot(
                            near, face_t[2 * whole + face], preferred_element_type=jnp.float32
                        )
                    owned[group, cell] = total

    def merge(group):
        @pl.when(is_first)
        def _():
            whole_wait(inbox.at[group, remote], inbox_sems.at[group])

        @pl.when(section > 0)
        def _():
            whole_wait(inbox.at[group], inbox_sems.at[group])

        messages = inbox[group].reshape(span * MSG, LANES)
        summed = jnp.dot(selector[group], messages, preferred_element_type=jnp.float32)
        total = owned[group] + summed.reshape(cell_grp, R, LANES)
        merged[group] = total.astype(jnp.bfloat16)

    def send_partials(group):
        order_x = sorted(range(span_x), key=lambda x: -min(x, span_x - x))

        @pl.loop(0, span_y // 2)
        def _(index):
            turns = []
            for y in (span_y // 2 + index, span_y // 2 - 1 - index):
                for x in order_x:
                    turns.append(x * span_y + y)
            for turn in turns:
                for place in range(CAP):
                    column = group * CAP + place
                    piece = slots_next[turn, column]
                    near = merged[group, slots_next[turn, GROUPS * CAP + column]]
                    term = next_rhs[piece].astype(jnp.float32) - jnp.dot(
                        near, coupling[piece], preferred_element_type=jnp.float32
                    )
                    outbox[group, turn, pl.ds(place * R, R), :] = term.astype(jnp.bfloat16)
                pltpu.make_async_remote_copy(
                    src_ref=outbox.at[group, turn],
                    dst_ref=inbox.at[group, turn],
                    send_sem=outbox_sems.at[group],
                    recv_sem=inbox_sems.at[group],
                    device_id={"stream": after, "span": peer(turn)},
                    device_id_type=MESH,
                ).start()

    def solve(group):
        for half in range(cell_grp // HALF):
            for j in range(HALF):
                cell = half * HALF + j
                sent[group, cell] = jnp.dot(
                    merged[group, cell],
                    inverse_t[group * cell_grp + cell],
                    preferred_element_type=jnp.float32,
                ).astype(jnp.bfloat16)

            @pl.when(jnp.logical_not(is_last))
            def _():
                downstream(group, half).start()

    for group in range(GROUPS):
        own_terms(group)
        merge(group)

        @pl.when(jnp.logical_not(is_last))
        def _():
            send_partials(group)

        solve(group)

    for group in range(GROUPS):
        out[pl.ds(group * cell_grp, cell_grp)] = sent[group, :, :, :U]

    whole_wait(index_out.at[remote], index_sems.at[0])

    @pl.when(section > 0)
    def _():
        for copy in shipments():
            copy.wait_send()

    @pl.when(is_first)
    def _():
        for group in range(GROUPS):
            whole_wait(first_box.at[group, remote], first_sems.at[group])

    @pl.when(jnp.logical_not(is_last))
    def _():
        for group in range(GROUPS):
            whole_wait(outbox.at[group], outbox_sems.at[group])
            whole_wait(sent.at[group], sent_sems.at[group])


def on_device(
    sizes,
    right_side,
    up_blocks,
    inverses,
    up_cells,
    piece_rhs,
    piece_blocks,
    piece_up,
    piece_owner,
    piece_cell,
):
    sections, span_x, span_y, cells, slots = sizes
    span = span_x * span_y
    cell_grp = cells // GROUPS
    vmem = pl.BlockSpec(memory_space=pltpu.VMEM)
    smem = pl.BlockSpec(memory_space=pltpu.SMEM)
    bf16 = jnp.bfloat16
    states = pl.pallas_call(
        functools.partial(section_kernel, sizes),
        out_shape=jax.ShapeDtypeStruct((cells, R, U), bf16),
        in_specs=[smem] + [vmem] * 8,
        out_specs=vmem,
        scratch_shapes=[
            pltpu.VMEM((2 * cells, LANES, LANES), bf16),
            pltpu.VMEM((cells, LANES, LANES), bf16),
            pltpu.VMEM((slots, LANES, LANES), bf16),
            pltpu.VMEM((cells, R, LANES), bf16),
            pltpu.VMEM((slots, R, LANES), bf16),
            pltpu.VMEM((slots, LANES, LANES), bf16),
            pltpu.VMEM((slots, R, LANES), bf16),
            pltpu.VMEM((slots, LANES, LANES), bf16),
            pltpu.VMEM((span, LANES), jnp.int32),
            pltpu.VMEM((span, LANES), jnp.int32),
            pltpu.SMEM((span, LANES), jnp.int32),
            pltpu.SMEM((span, LANES), jnp.int32),
            pltpu.VMEM((span, GROUPS, LANES), jnp.int32),
            pltpu.VMEM((span, GROUPS, LANES), jnp.int32),
            pltpu.VMEM((GROUPS, cell_grp * R, span * MSG), bf16),
            pltpu.VMEM((GROUPS, span, MSG, LANES), bf16),
            pltpu.VMEM((GROUPS, span, MSG, LANES), bf16),
            pltpu.VMEM((GROUPS, span, MSG, LANES), bf16),
            pltpu.VMEM((cell_grp, R, LANES), bf16),
            pltpu.VMEM((cell_grp, R, LANES), bf16),
            pltpu.VMEM((GROUPS, cell_grp, R, LANES), bf16),
            pltpu.VMEM((GROUPS, cell_grp, R, LANES), jnp.float32),
            pltpu.VMEM((GROUPS, cell_grp, R, LANES), bf16),
            pltpu.SemaphoreType.DMA((2,)),
            pltpu.SemaphoreType.DMA((3,)),
            pltpu.SemaphoreType.DMA((3,)),
            pltpu.SemaphoreType.DMA((2,)),
            pltpu.SemaphoreType.DMA((GROUPS,)),
            pltpu.SemaphoreType.DMA((GROUPS,)),
            pltpu.SemaphoreType.DMA((GROUPS,)),
            pltpu.SemaphoreType.DMA((GROUPS,)),
            pltpu.SemaphoreType.DMA((GROUPS,)),
        ],
        compiler_params=pltpu.CompilerParams(
            collective_id=0, has_side_effects=True, vmem_limit_bytes=48 * 1024 * 1024
        ),
    )(
        up_cells[0],
        piece_owner.reshape(1, slots),
        piece_cell.reshape(1, slots),
        piece_up.reshape(1, slots),
        right_side.reshape(cells, U, R).swapaxes(1, 2),
        piece_rhs.reshape(slots, U, R).swapaxes(1, 2),
        up_blocks.reshape(2 * cells, U, U),
        inverses.reshape(cells, U, U),
        piece_blocks.reshape(slots, U, U),
    )
    return states.swapaxes(1, 2).reshape(1, cells, U * R)


def solution(mesh):
    sections, span = mesh.shape["stream"], mesh.shape["span"]
    span_x = 4 if span == 32 else 2
    sizes = (sections, span_x, span // span_x, 56, 48)
    in_specs = (
        P("stream", "span", None),
        P("stream", "span", None),
        P("stream", "span", None),
        P("stream", "span", None),
        P("stream", "span", None),
        P("stream", "span", None),
        P("stream", "span"),
        P("stream", "span", None),
        P("stream", "span"),
    )
    out_specs = P("stream", "span", None)
    return jax.shard_map(
        functools.partial(on_device, sizes),
        mesh=mesh,
        in_specs=in_specs,
        out_specs=out_specs,
        check_vma=False,
    )
```

time: 223 us -> 194 us (0.87)
  Pallas kernels: 204 us -> 176 us
    pallas_call x1, Pallas kernels: 204 us -> 176 us  [on_device(): pl.pallas_call(functools.partial(section_kernel, sizes), out_shape=jax.Sh...]
where the time goes in v2:
time: 194 us
  Pallas kernels  176 us (91%)
  local copies, waits for them, and re-layouts  18.1 us (9%)
    pallas_call x1, Pallas kernels, on_device(): pl.pallas_call(functools.partial(section_kernel, sizes), out_shape=jax.Sh...  176 us
    reshape x1, local copies, waits for them, and re-layouts, on_device(): up_blocks.reshape(2 * cells, U, U)  7.81 us

profile of v2, /device:TPU:449, one launch (start us, length us, event | category | flops | bytes accessed | tf_op | source)
XLA Modules:
  0.0 193.7 jit_solution(8199459808768572555)
XLA Ops:
  0.0 0.0 copy-start.3
  0.0 0.8 copy.15.up_cells
  0.9 1.2 copy.11
  2.0 0.5 copy.12
  2.6 1.2 copy.13
  3.7 0.5 copy.14
  4.2 0.0 copy-done.3
  4.2 1.6 reshape.26.piece_blocks
  5.9 3.1 %reshape.25.inverses = bf16[56,100,100]{2,1,0:T(8,128)(2,1)S(1)} reshape(bf16[1,56,10000]{2,1,0:T(8,128)(2,1)} %param.11) | data formatting | bytes 2240000 | tf_op jit(solution)/shard_map/reshape | solution.py:440
  9.0 0.0 copy-start
  9.0 0.0 copy-start.1
  9.0 0.0 copy-start.2
  9.0 7.8 %reshape.24.up_blocks = bf16[112,100,100]{2,1,0:T(8,128)(2,1)} reshape(bf16[1,56,20000]{2,1,0:T(8,128)(2,1)} %param.10) | data formatting | bytes 4480000 | tf_op jit(solution)/shard_map/reshape | solution.py:439
  16.9 0.0 copy-done
  16.9 0.0 copy-done.1
  16.9 0.0 copy-done.2
  16.9 175.5 %shard_map.91 = bf16[56,16,100]{2,1,0:T(8,128)(2,1)S(1)} custom-call(s32[56,2]{1,0:T(8,128)S(1)} %copy.15.up_cells, s32[1,48]{1,0:T(1,128)S(1)} %bitcast.11, s32[1,48]{1,0:T(1,128)S(1)} %copy-done.1, s32[1,48]{1,0:T(1,128)S(1)} %copy-done.2, bf16[56,16,100]{2,1,0:T(8,128)(2,1)S(1)} %bitcast.8, bf16[48,16,100]{2,1,0:T(8,128)(2,1)S(1)} %bitcast.10, ...), custom_call_target="tpu_custom_call" | custom-call | tf_op jit(solution)/shard_map/pallas_call | solution.py:390
  192.4 0.5 copy.16
  192.9 0.9 copy.17
Async XLA Ops:
  0.0 4.2 %copy-start.3 = (bf16[1,48,10000]{2,1,0:T(8,128)(2,1)S(1)}, bf16[1,48,10000]{2,1,0:T(8,128)(2,1)}, u32[]{:S(2)}) copy-start(bf16[1,48,10000]{2,1,0:T(8,128)(2,1)} %param.14) | copy-start | bytes 2880004
  9.0 7.8 %copy-start = (s32[1,48,1]{1,2,0:T(1,128)S(1)}, s32[1,48,1]{1,2,0:T(1,128)}, u32[]{:S(2)}) copy-start(s32[1,48,1]{1,2,0:T(1,128)} %param.16) | copy-start | bytes 580
  9.0 7.8 %copy-start.1 = (s32[1,48]{1,0:T(1,128)S(1)}, s32[1,48]{1,0:T(1,128)}, u32[]{:S(2)}) copy-start(s32[1,48]{1,0:T(1,128)} %cell_row.1) | copy-start | bytes 580
  9.0 7.8 %copy-start.2 = (s32[1,48]{1,0:T(1,128)S(1)}, s32[1,48]{1,0:T(1,128)}, u32[]{:S(2)}) copy-start(s32[1,48]{1,0:T(1,128)} %up_row.1) | copy-start | bytes 580

commit v3 on v2

--- a/solution.py
+++ b/solution.py
@@ -16,6 +16,8 @@
 BLOCK = 4
 HALF = 14
 UP_LANE = 64
+STRIDE = 136
+FIRST_ROWS = 32
 MESH = pl.DeviceIdType.MESH
 
 
@@ -37,12 +39,14 @@
     inverses,
     piece_blocks,
     out,
+    face_flat,
+    inverse_flat,
+    piece_flat,
+    spread,
     face_t,
     inverse_t,
-    piece_pad,
     rhs_pad,
     piece_rhs_pad,
-    next_piece,
     next_rhs,
     coupling,
     table,
@@ -60,6 +64,7 @@
     sent,
     owned,
     merged,
+    load_sems,
     table_sems,
     ship_sems,
     ship_recv_sems,
@@ -78,16 +83,28 @@
     me_x, me_y = me // span_y, me % span_y
     after, ahead = (section + 1) % sections, (section + sections - 1) % sections
     arrived = (arrived_0, arrived_1)
-    remote = pl.ds(1, span - 1)
+    near = span // 2
+    others = pl.ds(0, span - 1)
     is_first, is_last = section == 0, section == sections - 1
 
+    order_x = sorted(range(span_x), key=lambda x: -min(x, span_x - x))
+
     def peer(turn):
-        x = (me_x + turn // span_y) % span_x
-        y = (me_y + turn % span_y) % span_y
-        return x * span_y + y
+        pair, place = turn // (2 * span_x), turn % span_x
+        upper = turn // span_x % 2 == 0
+        y = jnp.where(upper, span_y // 2 + pair, span_y // 2 - 1 - pair)
+        x = sum(order_x[i] * jnp.where(place == i, 1, 0) for i in range(span_x))
+        return (me_x + x) % span_x * span_y + (me_y + y) % span_y
 
     def whole_wait(ref, sem):
         pltpu.make_async_copy(ref, ref, sem).wait()
+
+    loads = [
+        pltpu.make_async_copy(inverses, inverse_flat, load_sems.at[0]),
+        pltpu.make_async_copy(up_blocks, face_flat, load_sems.at[1]),
+    ]
+    for load in loads:
+        load.start()
 
     barrier = pltpu.get_barrier_semaphore()
 
@@ -100,7 +117,7 @@
             device_id_type=MESH,
         )
 
-    @pl.loop(1, span)
+    @pl.loop(0, span - 1)
     def _(turn):
         pl.semaphore_signal(barrier, inc=1, device_id={"span": peer(turn)}, device_id_type=MESH)
 
@@ -142,20 +159,40 @@
         def _(i):
             target[i, : source.shape[1], : source.shape[2]] = source[i]
 
-    def transposed(target, count):
+    def unfolded(flat, offset, base, count):
+        def tile(block, height):
+            for i in range(U):
+                start = offset + U * i
+                rows = flat[pl.ds(block, height), start : start + U]
+                spread[pl.ds(block * STRIDE + i, height, stride=STRIDE), :U] = rows.astype(
+                    jnp.float32
+                )
+
+        @pl.loop(0, count // 16)
+        def _(index):
+            tile(pl.multiple_of(base + index * 16, 16), 16)
+
+        if count % 16:
+            tile(base + count // 16 * 16, count % 16)
+
+    def matrix(block):
+        return spread[pl.ds(block * STRIDE, LANES), :]
+
+    def transposed(target, base, count):
         @pl.loop(0, count // BLOCK)
         def _(index):
             for j in range(BLOCK):
-                i = index * BLOCK + j
-                target[i] = target[i].astype(jnp.float32).T.astype(jnp.bfloat16)
-
+                block = index * BLOCK + j
+                target[base + block] = matrix(block).T.astype(jnp.bfloat16)
+
+    spread[...] = jnp.zeros_like(spread)
     padded(piece_rhs, piece_rhs_pad, slots)
-    padded(piece_blocks, piece_pad, slots)
     padded(right_side, rhs_pad, cells)
 
     pl.semaphore_wait(barrier, 2 * span)
 
     def shipments():
+        parts = (pl.ds(0, FIRST_ROWS), pl.ds(FIRST_ROWS, slots - FIRST_ROWS))
         return [
             pltpu.make_async_remote_copy(
                 src_ref=source,
@@ -166,7 +203,12 @@
                 device_id_type=MESH,
             )
             for i, (source, target) in enumerate(
-                ((table, next_table), (piece_rhs_pad, next_rhs), (piece_pad, next_piece))
+                (
+                    (table, next_table),
+                    (piece_blocks.at[parts[0]], piece_flat.at[parts[0]]),
+                    (piece_rhs_pad, next_rhs),
+                    (piece_blocks.at[parts[1]], piece_flat.at[parts[1]]),
+                )
             )
         ]
 
@@ -175,9 +217,9 @@
         for copy in shipments():
             copy.start()
 
-    index_in[0] = index_out[0]
-
-    @pl.loop(1, span)
+    index_in[span - 1] = index_out[span - 1]
+
+    @pl.loop(0, span - 1)
     def _(turn):
         pltpu.make_async_remote_copy(
             src_ref=index_out.at[turn],
@@ -193,10 +235,10 @@
         pltpu.make_async_copy(table, own_slots, table_sems.at[0]).wait()
         for group in range(GROUPS):
             for place in range(CAP):
-                piece = own_slots[0, group * CAP + place]
-                inbox[group, 0, pl.ds(place * R, R), :] = piece_rhs_pad[piece]
-
-            @pl.loop(1, span)
+                piece = own_slots[span - 1, group * CAP + place]
+                inbox[group, span - 1, pl.ds(place * R, R), :] = piece_rhs_pad[piece]
+
+            @pl.loop(0, span - 1)
             def _(turn):
                 for place in range(CAP):
                     piece = own_slots[turn, group * CAP + place]
@@ -205,39 +247,52 @@
                     src_ref=first_box.at[group, turn],
                     dst_ref=inbox.at[group, turn],
                     send_sem=first_sems.at[group],
-                    recv_sem=inbox_sems.at[group],
+                    recv_sem=inbox_sems.at[group, turn // near],
                     device_id={"span": peer(turn)},
                     device_id_type=MESH,
                 ).start()
 
-    padded(inverses, inverse_t, cells)
-    transposed(inverse_t, cells)
+    loads[0].wait()
+    unfolded(inverse_flat, 0, 0, cells)
+    transposed(inverse_t, 0, cells)
 
     @pl.when(jnp.logical_not(is_last))
     def _():
         whole_wait(next_table, ship_recv_sems.at[0])
         to_slots = pltpu.make_async_copy(next_table, slots_next, table_sems.at[1])
         to_slots.start()
-        whole_wait(next_rhs, ship_recv_sems.at[1])
-        whole_wait(next_piece, ship_recv_sems.at[2])
         to_slots.wait()
         for group in range(GROUPS):
-
-            @pl.loop(0, slot_grp // BLOCK)
+            base = group * slot_grp
+            if group == 0:
+                whole_wait(piece_flat.at[pl.ds(0, FIRST_ROWS)], ship_recv_sems.at[1])
+                unfolded(piece_flat, 0, 0, FIRST_ROWS)
+            else:
+                whole_wait(
+                    piece_flat.at[pl.ds(FIRST_ROWS, slots - FIRST_ROWS)], ship_recv_sems.at[3]
+                )
+                unfolded(piece_flat, 0, FIRST_ROWS, slots - FIRST_ROWS)
+
+            @pl.loop(0, slot_grp // 8)
             def _(index):
-                for j in range(BLOCK):
-                    piece = group * slot_grp + index * BLOCK + j
-                    cell = group * cell_grp + slots_next[0, UP_LANE + piece]
-                    coupling[piece] = times_transposed(inverse_t[cell], next_piece[piece]).astype(
-                        jnp.bfloat16
-                    )
+                for j in range(8):
+                    block = index * 8 + j
+                    cell = group * cell_grp + slots_next[0, UP_LANE + base + block]
+                    coupling[base + block] = times_transposed(
+                        inverse_t[cell], matrix(base + block).astype(jnp.bfloat16)
+                    ).astype(jnp.bfloat16)
+
+        whole_wait(next_rhs, ship_recv_sems.at[2])
+
+    loads[1].wait()
 
     @pl.when(section > 0)
     def _():
-        padded(up_blocks, face_t, 2 * cells)
-        transposed(face_t, 2 * cells)
-
-    whole_wait(index_in.at[remote], index_sems.at[1])
+        for face in range(2):
+            unfolded(face_flat, face * U * U, 0, cells)
+            transposed(face_t, face * cells, cells)
+
+    whole_wait(index_in.at[others], index_sems.at[1])
     row = lax.broadcasted_iota(jnp.int32, (cell_grp * R, LANES), 0)
     column = lax.broadcasted_iota(jnp.int32, (cell_grp * R, LANES), 1)
     same_side = row % R == column % R
@@ -247,7 +302,8 @@
             for j in range(1, BLOCK):
                 named = named + index_in[BLOCK * part + j, pl.ds(group, 1), :]
             hit = same_side & (row // R + 1 == named)
-            selector[group, :, pl.ds(part * LANES, LANES)] = hit.astype(jnp.bfloat16)
+            half, place = divmod(part * BLOCK, near)
+            selector[group, half, :, pl.ds(place * MSG, LANES)] = hit.astype(jnp.bfloat16)
 
     def downstream(group, half):
         cells_of = pl.ds(half * HALF, HALF)
@@ -276,49 +332,52 @@
                     whole = group * cell_grp + cell
                     total = rhs_pad[whole].astype(jnp.float32)
                     for face in range(2):
-                        near = arrived[group][up_cells[whole, face]]
+                        state = arrived[group][up_cells[face, whole]]
                         total = total - jnp.dot(
-                            near, face_t[2 * whole + face], preferred_element_type=jnp.float32
+                            state, face_t[face * cells + whole], preferred_element_type=jnp.float32
                         )
                     owned[group, cell] = total
 
     def merge(group):
-        @pl.when(is_first)
-        def _():
-            whole_wait(inbox.at[group, remote], inbox_sems.at[group])
-
-        @pl.when(section > 0)
-        def _():
-            whole_wait(inbox.at[group], inbox_sems.at[group])
-
-        messages = inbox[group].reshape(span * MSG, LANES)
-        summed = jnp.dot(selector[group], messages, preferred_element_type=jnp.float32)
-        total = owned[group] + summed.reshape(cell_grp, R, LANES)
-        merged[group] = total.astype(jnp.bfloat16)
+        total = owned[group]
+        for half, part in ((1, pl.ds(near, near)), (0, pl.ds(0, near))):
+
+            @pl.when(is_first)
+            def _():
+                known = pl.ds(near, near - 1) if half else part
+                whole_wait(inbox.at[group, known], inbox_sems.at[group, half])
+
+            @pl.when(section > 0)
+            def _():
+                whole_wait(inbox.at[group, part], inbox_sems.at[group, half])
+
+            messages = inbox[group, part].reshape(near * MSG, LANES)
+            summed = jnp.dot(
+                selector[group, half], messages, preferred_element_type=jnp.float32
+            ).reshape(cell_grp, R, LANES)
+            if half:
+                owned[group] = total + summed
+            else:
+                merged[group] = (owned[group] + summed).astype(jnp.bfloat16)
 
     def send_partials(group):
-        order_x = sorted(range(span_x), key=lambda x: -min(x, span_x - x))
-
-        @pl.loop(0, span_y // 2)
+        @pl.loop(0, span // 8)
         def _(index):
-            turns = []
-            for y in (span_y // 2 + index, span_y // 2 - 1 - index):
-                for x in order_x:
-                    turns.append(x * span_y + y)
-            for turn in turns:
+            for j in range(8):
+                turn = index * 8 + j
                 for place in range(CAP):
                     column = group * CAP + place
                     piece = slots_next[turn, column]
-                    near = merged[group, slots_next[turn, GROUPS * CAP + column]]
+                    state = merged[group, slots_next[turn, GROUPS * CAP + column]]
                     term = next_rhs[piece].astype(jnp.float32) - jnp.dot(
-                        near, coupling[piece], preferred_element_type=jnp.float32
+                        state, coupling[piece], preferred_element_type=jnp.float32
                     )
                     outbox[group, turn, pl.ds(place * R, R), :] = term.astype(jnp.bfloat16)
                 pltpu.make_async_remote_copy(
                     src_ref=outbox.at[group, turn],
                     dst_ref=inbox.at[group, turn],
                     send_sem=outbox_sems.at[group],
-                    recv_sem=inbox_sems.at[group],
+                    recv_sem=inbox_sems.at[group, turn // near],
                     device_id={"stream": after, "span": peer(turn)},
                     device_id_type=MESH,
                 ).start()
@@ -350,7 +409,7 @@
     for group in range(GROUPS):
         out[pl.ds(group * cell_grp, cell_grp)] = sent[group, :, :, :U]
 
-    whole_wait(index_out.at[remote], index_sems.at[0])
+    whole_wait(index_out.at[others], index_sems.at[0])
 
     @pl.when(section > 0)
     def _():
@@ -360,7 +419,7 @@
     @pl.when(is_first)
     def _():
         for group in range(GROUPS):
-            whole_wait(first_box.at[group, remote], first_sems.at[group])
+            whole_wait(first_box.at[group, others], first_sems.at[group])
 
     @pl.when(jnp.logical_not(is_last))
     def _():
@@ -390,15 +449,17 @@
     states = pl.pallas_call(
         functools.partial(section_kernel, sizes),
         out_shape=jax.ShapeDtypeStruct((cells, R, U), bf16),
-        in_specs=[smem] + [vmem] * 8,
+        in_specs=[smem] + [vmem] * 5 + [pl.BlockSpec(memory_space=pl.ANY)] * 3,
         out_specs=vmem,
         scratch_shapes=[
+            pltpu.VMEM((cells, 2 * U * U), bf16),
+            pltpu.VMEM((cells, U * U), bf16),
+            pltpu.VMEM((slots, U * U), bf16),
+            pltpu.VMEM((cells * STRIDE, LANES), jnp.float32),
             pltpu.VMEM((2 * cells, LANES, LANES), bf16),
             pltpu.VMEM((cells, LANES, LANES), bf16),
-            pltpu.VMEM((slots, LANES, LANES), bf16),
             pltpu.VMEM((cells, R, LANES), bf16),
             pltpu.VMEM((slots, R, LANES), bf16),
-            pltpu.VMEM((slots, LANES, LANES), bf16),
             pltpu.VMEM((slots, R, LANES), bf16),
             pltpu.VMEM((slots, LANES, LANES), bf16),
             pltpu.VMEM((span, LANES), jnp.int32),
@@ -407,7 +468,7 @@
             pltpu.SMEM((span, LANES), jnp.int32),
             pltpu.VMEM((span, GROUPS, LANES), jnp.int32),
             pltpu.VMEM((span, GROUPS, LANES), jnp.int32),
-            pltpu.VMEM((GROUPS, cell_grp * R, span * MSG), bf16),
+            pltpu.VMEM((GROUPS, 2, cell_grp * R, span // 2 * MSG), bf16),
             pltpu.VMEM((GROUPS, span, MSG, LANES), bf16),
             pltpu.VMEM((GROUPS, span, MSG, LANES), bf16),
             pltpu.VMEM((GROUPS, span, MSG, LANES), bf16),
@@ -417,12 +478,13 @@
             pltpu.VMEM((GROUPS, cell_grp, R, LANES), jnp.float32),
             pltpu.VMEM((GROUPS, cell_grp, R, LANES), bf16),
             pltpu.SemaphoreType.DMA((2,)),
-            pltpu.SemaphoreType.DMA((3,)),
-            pltpu.SemaphoreType.DMA((3,)),
+            pltpu.SemaphoreType.DMA((2,)),
+            pltpu.SemaphoreType.DMA((4,)),
+            pltpu.SemaphoreType.DMA((4,)),
             pltpu.SemaphoreType.DMA((2,)),
             pltpu.SemaphoreType.DMA((GROUPS,)),
             pltpu.SemaphoreType.DMA((GROUPS,)),
-            pltpu.SemaphoreType.DMA((GROUPS,)),
+            pltpu.SemaphoreType.DMA((GROUPS, 2)),
             pltpu.SemaphoreType.DMA((GROUPS,)),
             pltpu.SemaphoreType.DMA((GROUPS,)),
         ],
@@ -430,15 +492,15 @@
             collective_id=0, has_side_effects=True, vmem_limit_bytes=48 * 1024 * 1024
         ),
     )(
-        up_cells[0],
+        up_cells[0].T,
         piece_owner.reshape(1, slots),
         piece_cell.reshape(1, slots),
         piece_up.reshape(1, slots),
         right_side.reshape(cells, U, R).swapaxes(1, 2),
         piece_rhs.reshape(slots, U, R).swapaxes(1, 2),
-        up_blocks.reshape(2 * cells, U, U),
-        inverses.reshape(cells, U, U),
-        piece_blocks.reshape(slots, U, U),
+        up_blocks.reshape(cells, 2 * U * U),
+        inverses.reshape(cells, U * U),
+        piece_blocks.reshape(slots, U * U),
     )
     return states.swapaxes(1, 2).reshape(1, cells, U * R)
 

time: 194 us -> 177 us (0.912)
  local copies, waits for them, and re-layouts: 18.1 us -> 7.3 us
  Pallas kernels: 176 us -> 170 us
    reshape x3 -> x0, local copies, waits for them, and re-layouts: 12.6 us -> none  [the longest x1 7.81 us: on_device(): up_blocks.reshape(2 * cells, U, U)]
    pallas_call x1, Pallas kernels: 176 us -> 170 us  [on_device(): pl.pallas_call(functools.partial(section_kernel, sizes), out_shape=jax.Sh...]
    unnamed x10 -> x16, local copies, waits for them, and re-layouts: 2.36 us -> 4.95 us
where the time goes in v3:
time: 177 us
  Pallas kernels  170 us (96%)
  local copies, waits for them, and re-layouts  7.3 us (4%)
    pallas_call x1, Pallas kernels, on_device(): pl.pallas_call(functools.partial(section_kernel, sizes), out_shape=jax.Sh...  170 us
    unnamed x16, local copies, waits for them, and re-layouts  4.95 us

profile of v3, /device:TPU:449, one launch (start us, length us, event | category | flops | bytes accessed | tf_op | source)
XLA Modules:
  0.0 177.2 jit_solution(9138575643286513642)
XLA Ops:
  0.0 0.0 copy-start.5
  0.0 0.0 copy-start.4
  0.0 0.0 copy-start.6
  0.0 0.0 copy-start.3
  0.0 0.0 copy-start
  0.0 1.3 copy.10
  1.4 0.5 copy.11
  1.9 1.2 copy.12
  3.0 0.5 copy.13
  3.6 0.0 copy-done.5
  3.6 0.0 copy-done.4
  3.6 0.0 copy-done.6
  3.6 0.0 copy-done.3
  3.6 0.0 copy-done
  3.6 0.0 copy-start.1
  3.6 1.2 copy-done.1
  4.9 0.0 copy-start.2
  4.9 1.2 copy-done.2
  6.1 169.8 %shard_map.91 = bf16[56,16,100]{2,1,0:T(8,128)(2,1)S(1)} custom-call(s32[2,56]{1,0:T(2,128)S(1)} %bitcast.19, s32[1,48]{1,0:T(1,128)S(1)} %bitcast.20, s32[1,48]{1,0:T(1,128)S(1)} %copy-done.5, s32[1,48]{1,0:T(1,128)S(1)} %copy-done.6, bf16[56,16,100]{2,1,0:T(8,128)(2,1)S(1)} %bitcast.16, bf16[48,16,100]{2,1,0:T(8,128)(2,1)S(1)} %bitcast.18, ...), custom_call_target="tpu_custom_call" | custom-call | tf_op jit(solution)/shard_map/pallas_call | solution.py:449
  175.9 0.5 copy.14
  176.4 0.9 copy.15
Async XLA Ops:
  0.0 3.6 %copy-start.5 = (s32[1,48]{1,0:T(1,128)S(1)}, s32[1,48]{1,0:T(1,128)}, u32[]{:S(2)}) copy-start(s32[1,48]{1,0:T(1,128)} %cell_row.1) | copy-start | bytes 580
  0.0 3.6 %copy-start.4 = (s32[1,48,1]{1,2,0:T(1,128)S(1)}, s32[1,48,1]{1,2,0:T(1,128)}, u32[]{:S(2)}) copy-start(s32[1,48,1]{1,2,0:T(1,128)} %param.16) | copy-start | bytes 580
  0.0 3.6 %copy-start.6 = (s32[1,48]{1,0:T(1,128)S(1)}, s32[1,48]{1,0:T(1,128)}, u32[]{:S(2)}) copy-start(s32[1,48]{1,0:T(1,128)} %up_row.1) | copy-start | bytes 580
  0.0 3.6 %copy-start.3 = (s32[1,56,2]{1,2,0:T(2,128)S(1)}, s32[1,56,2]{1,2,0:T(2,128)}, u32[]{:S(2)}) copy-start(s32[1,56,2]{1,2,0:T(2,128)} %param.12) | copy-start | bytes 1348
  0.0 3.6 %copy-start = (bf16[1,56,20000]{2,1,0:T(8,128)(2,1)S(1)}, bf16[1,56,20000]{2,1,0:T(8,128)(2,1)}, u32[]{:S(2)}) copy-start(bf16[1,56,20000]{2,1,0:T(8,128)(2,1)} %param.10) | copy-start | bytes 6720004
  3.6 1.3 copy-start.1
  4.9 1.2 copy-start.2

commit v4 on v3

--- a/solution.py
+++ b/solution.py
@@ -47,7 +47,8 @@
     inverse_t,
     rhs_pad,
     piece_rhs_pad,
-    next_rhs,
+    next_rhs_0,
+    next_rhs_1,
     coupling,
     table,
     next_table,
@@ -80,9 +81,10 @@
     cell_grp, slot_grp = cells // GROUPS, slots // GROUPS
     section = lax.axis_index("stream")
     me = lax.axis_index("span")
-    me_x, me_y = me // span_y, me % span_y
-    after, ahead = (section + 1) % sections, (section + sections - 1) % sections
+    me_x, me_y = lax.div(me, span_y), lax.rem(me, span_y)
+    after, ahead = lax.rem(section + 1, sections), lax.rem(section + sections - 1, sections)
     arrived = (arrived_0, arrived_1)
+    next_rhs = (next_rhs_0, next_rhs_1)
     near = span // 2
     others = pl.ds(0, span - 1)
     is_first, is_last = section == 0, section == sections - 1
@@ -96,6 +98,23 @@
         x = sum(order_x[i] * jnp.where(place == i, 1, 0) for i in range(span_x))
         return (me_x + x) % span_x * span_y + (me_y + y) % span_y
 
+    pairs, places = span_y // 2, 2 * span_x
+    row_of = [lax.rem(me_x + x, span_x) * span_y for x in order_x]
+
+    def peer_at(pair, place):
+        y = span_y // 2 + pair if place < span_x else span_y // 2 - 1 - pair
+        return row_of[place % span_x] + lax.rem(me_y + y, span_y)
+
+    def for_others(act):
+        @pl.loop(0, pairs)
+        def _(pair):
+            for place in range(places - 1):
+                act(pair * places + place, peer_at(pair, place))
+
+            @pl.when(pair < pairs - 1)
+            def _():
+                act(pair * places + places - 1, peer_at(pair, places - 1))
+
     def whole_wait(ref, sem):
         pltpu.make_async_copy(ref, ref, sem).wait()
 
@@ -108,19 +127,20 @@
 
     barrier = pltpu.get_barrier_semaphore()
 
-    @pl.loop(0, span)
-    def _(turn):
-        pl.semaphore_signal(
-            barrier,
-            inc=1,
-            device_id={"stream": ahead, "span": peer(turn)},
-            device_id_type=MESH,
-        )
-
-    @pl.loop(0, span - 1)
-    def _(turn):
-        pl.semaphore_signal(barrier, inc=1, device_id={"span": peer(turn)}, device_id_type=MESH)
-
+    def greet(turn, device):
+        pl.semaphore_signal(barrier, inc=1, device_id={"span": device}, device_id_type=MESH)
+
+    @pl.loop(0, pairs)
+    def _(pair):
+        for place in range(places):
+            pl.semaphore_signal(
+                barrier,
+                inc=1,
+                device_id={"stream": ahead, "span": peer_at(pair, place)},
+                device_id_type=MESH,
+            )
+
+    for_others(greet)
     pl.semaphore_signal(barrier, inc=1, device_id={"stream": after}, device_id_type=MESH)
 
     turn_col = lax.broadcasted_iota(jnp.int32, (span, slots), 0)
@@ -189,10 +209,31 @@
     padded(piece_rhs, piece_rhs_pad, slots)
     padded(right_side, rhs_pad, cells)
 
+    loads[0].wait()
+    unfolded(inverse_flat, 0, 0, cells)
+    transposed(inverse_t, 0, cells)
+
+    loads[1].wait()
+
+    @pl.when(section > 0)
+    def _():
+        for face in range(2):
+            unfolded(face_flat, face * U * U, 0, cells)
+
+            @pl.loop(0, cells // BLOCK)
+            def _(index):
+                for j in range(BLOCK):
+                    cell = index * BLOCK + j
+                    face_t[cell, pl.ds(face * LANES, LANES), :] = matrix(cell).T.astype(
+                        jnp.bfloat16
+                    )
+
     pl.semaphore_wait(barrier, 2 * span)
 
+    halves = (pl.ds(0, slot_grp), pl.ds(slot_grp, slot_grp))
+    parts = (pl.ds(0, FIRST_ROWS), pl.ds(FIRST_ROWS, slots - FIRST_ROWS))
+
     def shipments():
-        parts = (pl.ds(0, FIRST_ROWS), pl.ds(FIRST_ROWS, slots - FIRST_ROWS))
         return [
             pltpu.make_async_remote_copy(
                 src_ref=source,
@@ -205,8 +246,9 @@
             for i, (source, target) in enumerate(
                 (
                     (table, next_table),
+                    (piece_rhs_pad.at[halves[0]], next_rhs[0]),
                     (piece_blocks.at[parts[0]], piece_flat.at[parts[0]]),
-                    (piece_rhs_pad, next_rhs),
+                    (piece_rhs_pad.at[halves[1]], next_rhs[1]),
                     (piece_blocks.at[parts[1]], piece_flat.at[parts[1]]),
                 )
             )
@@ -217,44 +259,47 @@
         for copy in shipments():
             copy.start()
 
-    index_in[span - 1] = index_out[span - 1]
-
-    @pl.loop(0, span - 1)
-    def _(turn):
+    def send_first(group):
+        def fill(box, turn):
+            for place in range(CAP):
+                piece = own_slots[turn, group * CAP + place]
+                box[group, turn, pl.ds(place * R, R), :] = piece_rhs_pad[piece]
+
+        def send(turn, device):
+            fill(first_box, turn)
+            pltpu.make_async_remote_copy(
+                src_ref=first_box.at[group, turn],
+                dst_ref=inbox.at[group, turn],
+                send_sem=first_sems.at[group],
+                recv_sem=inbox_sems.at[group, lax.div(turn, near)],
+                device_id={"span": device},
+                device_id_type=MESH,
+            ).start()
+
+        fill(inbox, span - 1)
+        for_others(send)
+
+    @pl.when(is_first)
+    def _():
+        pltpu.make_async_copy(table, own_slots, table_sems.at[0]).wait()
+        send_first(0)
+
+    def send_index(turn, device):
         pltpu.make_async_remote_copy(
             src_ref=index_out.at[turn],
             dst_ref=index_in.at[turn],
             send_sem=index_sems.at[0],
             recv_sem=index_sems.at[1],
-            device_id={"span": peer(turn)},
+            device_id={"span": device},
             device_id_type=MESH,
         ).start()
 
+    index_in[span - 1] = index_out[span - 1]
+    for_others(send_index)
+
     @pl.when(is_first)
     def _():
-        pltpu.make_async_copy(table, own_slots, table_sems.at[0]).wait()
-        for group in range(GROUPS):
-            for place in range(CAP):
-                piece = own_slots[span - 1, group * CAP + place]
-                inbox[group, span - 1, pl.ds(place * R, R), :] = piece_rhs_pad[piece]
-
-            @pl.loop(0, span - 1)
-            def _(turn):
-                for place in range(CAP):
-                    piece = own_slots[turn, group * CAP + place]
-                    first_box[group, turn, pl.ds(place * R, R), :] = piece_rhs_pad[piece]
-                pltpu.make_async_remote_copy(
-                    src_ref=first_box.at[group, turn],
-                    dst_ref=inbox.at[group, turn],
-                    send_sem=first_sems.at[group],
-                    recv_sem=inbox_sems.at[group, turn // near],
-                    device_id={"span": peer(turn)},
-                    device_id_type=MESH,
-                ).start()
-
-    loads[0].wait()
-    unfolded(inverse_flat, 0, 0, cells)
-    transposed(inverse_t, 0, cells)
+        send_first(1)
 
     @pl.when(jnp.logical_not(is_last))
     def _():
@@ -262,35 +307,22 @@
         to_slots = pltpu.make_async_copy(next_table, slots_next, table_sems.at[1])
         to_slots.start()
         to_slots.wait()
-        for group in range(GROUPS):
-            base = group * slot_grp
-            if group == 0:
-                whole_wait(piece_flat.at[pl.ds(0, FIRST_ROWS)], ship_recv_sems.at[1])
-                unfolded(piece_flat, 0, 0, FIRST_ROWS)
-            else:
-                whole_wait(
-                    piece_flat.at[pl.ds(FIRST_ROWS, slots - FIRST_ROWS)], ship_recv_sems.at[3]
-                )
-                unfolded(piece_flat, 0, FIRST_ROWS, slots - FIRST_ROWS)
-
-            @pl.loop(0, slot_grp // 8)
-            def _(index):
-                for j in range(8):
-                    block = index * 8 + j
-                    cell = group * cell_grp + slots_next[0, UP_LANE + base + block]
-                    coupling[base + block] = times_transposed(
-                        inverse_t[cell], matrix(base + block).astype(jnp.bfloat16)
-                    ).astype(jnp.bfloat16)
-
-        whole_wait(next_rhs, ship_recv_sems.at[2])
-
-    loads[1].wait()
-
-    @pl.when(section > 0)
-    def _():
-        for face in range(2):
-            unfolded(face_flat, face * U * U, 0, cells)
-            transposed(face_t, face * cells, cells)
+
+    def couple(group):
+        base = group * slot_grp
+        start, count = (0, FIRST_ROWS) if group == 0 else (FIRST_ROWS, slots - FIRST_ROWS)
+        whole_wait(next_rhs[group], ship_recv_sems.at[2 * group + 1])
+        whole_wait(piece_flat.at[parts[group]], ship_recv_sems.at[2 * group + 2])
+        unfolded(piece_flat, 0, start, count)
+
+        @pl.loop(0, slot_grp // 8)
+        def _(index):
+            for j in range(8):
+                block = base + index * 8 + j
+                cell = group * cell_grp + slots_next[0, UP_LANE + block]
+                coupling[block] = times_transposed(
+                    inverse_t[cell], matrix(block).astype(jnp.bfloat16)
+                ).astype(jnp.bfloat16)
 
     whole_wait(index_in.at[others], index_sems.at[1])
     row = lax.broadcasted_iota(jnp.int32, (cell_grp * R, LANES), 0)
@@ -305,6 +337,16 @@
             half, place = divmod(part * BLOCK, near)
             selector[group, half, :, pl.ds(place * MSG, LANES)] = hit.astype(jnp.bfloat16)
 
+    @pl.when(jnp.logical_not(is_last))
+    def _():
+        couple(0)
+
+    is_late = section <= 1
+
+    @pl.when(jnp.logical_not(is_last | is_late))
+    def _():
+        couple(1)
+
     def downstream(group, half):
         cells_of = pl.ds(half * HALF, HALF)
         return pltpu.make_async_remote_copy(
@@ -331,11 +373,12 @@
                     cell = index * 7 + j
                     whole = group * cell_grp + cell
                     total = rhs_pad[whole].astype(jnp.float32)
-                    for face in range(2):
-                        state = arrived[group][up_cells[face, whole]]
-                        total = total - jnp.dot(
-                            state, face_t[face * cells + whole], preferred_element_type=jnp.float32
-                        )
+                    states = jnp.concatenate(
+                        [arrived[group][up_cells[face, whole]] for face in range(2)], axis=1
+                    )
+                    total = total - jnp.dot(
+                        states, face_t[whole], preferred_element_type=jnp.float32
+                    )
                     owned[group, cell] = total
 
     def merge(group):
@@ -360,16 +403,16 @@
             else:
                 merged[group] = (owned[group] + summed).astype(jnp.bfloat16)
 
-    def send_partials(group):
-        @pl.loop(0, span // 8)
-        def _(index):
-            for j in range(8):
-                turn = index * 8 + j
+    def send_partials(group, first, last):
+        @pl.loop(first // places, last // places)
+        def _(pair):
+            for j in range(places):
+                turn = pair * places + j
                 for place in range(CAP):
                     column = group * CAP + place
                     piece = slots_next[turn, column]
                     state = merged[group, slots_next[turn, GROUPS * CAP + column]]
-                    term = next_rhs[piece].astype(jnp.float32) - jnp.dot(
+                    term = next_rhs[group][piece - group * slot_grp].astype(jnp.float32) - jnp.dot(
                         state, coupling[piece], preferred_element_type=jnp.float32
                     )
                     outbox[group, turn, pl.ds(place * R, R), :] = term.astype(jnp.bfloat16)
@@ -377,8 +420,8 @@
                     src_ref=outbox.at[group, turn],
                     dst_ref=inbox.at[group, turn],
                     send_sem=outbox_sems.at[group],
-                    recv_sem=inbox_sems.at[group, turn // near],
-                    device_id={"stream": after, "span": peer(turn)},
+                    recv_sem=inbox_sems.at[group, first // near],
+                    device_id={"stream": after, "span": peer_at(pair, j)},
                     device_id_type=MESH,
                 ).start()
 
@@ -397,14 +440,24 @@
                 downstream(group, half).start()
 
     for group in range(GROUPS):
+        if group == 1:
+
+            @pl.when(is_late)
+            def _():
+                couple(1)
+
         own_terms(group)
         merge(group)
 
         @pl.when(jnp.logical_not(is_last))
         def _():
-            send_partials(group)
+            send_partials(group, 0, near)
 
         solve(group)
+
+        @pl.when(jnp.logical_not(is_last))
+        def _():
+            send_partials(group, near, span)
 
     for group in range(GROUPS):
         out[pl.ds(group * cell_grp, cell_grp)] = sent[group, :, :, :U]
@@ -456,11 +509,12 @@
             pltpu.VMEM((cells, U * U), bf16),
             pltpu.VMEM((slots, U * U), bf16),
             pltpu.VMEM((cells * STRIDE, LANES), jnp.float32),
-            pltpu.VMEM((2 * cells, LANES, LANES), bf16),
+            pltpu.VMEM((cells, 2 * LANES, LANES), bf16),
             pltpu.VMEM((cells, LANES, LANES), bf16),
             pltpu.VMEM((cells, R, LANES), bf16),
             pltpu.VMEM((slots, R, LANES), bf16),
-            pltpu.VMEM((slots, R, LANES), bf16),
+            pltpu.VMEM((slots // GROUPS, R, LANES), bf16),
+            pltpu.VMEM((slots // GROUPS, R, LANES), bf16),
             pltpu.VMEM((slots, LANES, LANES), bf16),
             pltpu.VMEM((span, LANES), jnp.int32),
             pltpu.VMEM((span, LANES), jnp.int32),
@@ -479,8 +533,8 @@
             pltpu.VMEM((GROUPS, cell_grp, R, LANES), bf16),
             pltpu.SemaphoreType.DMA((2,)),
             pltpu.SemaphoreType.DMA((2,)),
-            pltpu.SemaphoreType.DMA((4,)),
-            pltpu.SemaphoreType.DMA((4,)),
+            pltpu.SemaphoreType.DMA((5,)),
+            pltpu.SemaphoreType.DMA((5,)),
             pltpu.SemaphoreType.DMA((2,)),
             pltpu.SemaphoreType.DMA((GROUPS,)),
             pltpu.SemaphoreType.DMA((GROUPS,)),

time: 177 us -> 177 us (level)
  no operation moved by 1% of the time
where the time goes in v4:
time: 177 us
  Pallas kernels  169 us (95%)
  local copies, waits for them, and re-layouts  7.3 us (4%)
    pallas_call x1, Pallas kernels, on_device(): pl.pallas_call(functools.partial(section_kernel, sizes), out_shape=jax.Sh...  169 us
    unnamed x16, local copies, waits for them, and re-layouts  4.95 us

profile of v4, /device:TPU:449, one launch (start us, length us, event | category | flops | bytes accessed | tf_op | source)
XLA Modules:
  0.0 176.9 jit_solution(16797325907466022291)
XLA Ops:
  0.0 0.0 copy-start.5
  0.0 0.0 copy-start.4
  0.0 0.0 copy-start.6
  0.0 0.0 copy-start.3
  0.0 0.0 copy-start
  0.0 1.3 copy.10
  1.4 0.5 copy.11
  1.9 1.2 copy.12
  3.0 0.5 copy.13
  3.6 0.0 copy-done.5
  3.6 0.0 copy-done.4
  3.6 0.0 copy-done.6
  3.6 0.0 copy-done.3
  3.6 0.0 copy-done
  3.6 0.0 copy-start.1
  3.6 1.2 copy-done.1
  4.9 0.0 copy-start.2
  4.9 1.2 copy-done.2
  6.1 169.4 %shard_map.91 = bf16[56,16,100]{2,1,0:T(8,128)(2,1)S(1)} custom-call(s32[2,56]{1,0:T(2,128)S(1)} %bitcast.19, s32[1,48]{1,0:T(1,128)S(1)} %bitcast.20, s32[1,48]{1,0:T(1,128)S(1)} %copy-done.5, s32[1,48]{1,0:T(1,128)S(1)} %copy-done.6, bf16[56,16,100]{2,1,0:T(8,128)(2,1)S(1)} %bitcast.16, bf16[48,16,100]{2,1,0:T(8,128)(2,1)S(1)} %bitcast.18, ...), custom_call_target="tpu_custom_call" | custom-call | tf_op jit(solution)/shard_map/pallas_call | solution.py:502
  175.5 0.5 copy.14
  176.0 0.9 copy.15
Async XLA Ops:
  0.0 3.6 %copy-start.5 = (s32[1,48]{1,0:T(1,128)S(1)}, s32[1,48]{1,0:T(1,128)}, u32[]{:S(2)}) copy-start(s32[1,48]{1,0:T(1,128)} %cell_row.1) | copy-start | bytes 580
  0.0 3.6 %copy-start.4 = (s32[1,48,1]{1,2,0:T(1,128)S(1)}, s32[1,48,1]{1,2,0:T(1,128)}, u32[]{:S(2)}) copy-start(s32[1,48,1]{1,2,0:T(1,128)} %param.16) | copy-start | bytes 580
  0.0 3.6 %copy-start.6 = (s32[1,48]{1,0:T(1,128)S(1)}, s32[1,48]{1,0:T(1,128)}, u32[]{:S(2)}) copy-start(s32[1,48]{1,0:T(1,128)} %up_row.1) | copy-start | bytes 580
  0.0 3.6 %copy-start.3 = (s32[1,56,2]{1,2,0:T(2,128)S(1)}, s32[1,56,2]{1,2,0:T(2,128)}, u32[]{:S(2)}) copy-start(s32[1,56,2]{1,2,0:T(2,128)} %param.12) | copy-start | bytes 1348
  0.0 3.6 %copy-start = (bf16[1,56,20000]{2,1,0:T(8,128)(2,1)S(1)}, bf16[1,56,20000]{2,1,0:T(8,128)(2,1)}, u32[]{:S(2)}) copy-start(bf16[1,56,20000]{2,1,0:T(8,128)(2,1)} %param.10) | copy-start | bytes 6720004
  3.6 1.3 copy-start.1
  4.9 1.2 copy-start.2

commit v5 on v4

--- a/solution.py
+++ b/solution.py
@@ -17,6 +17,7 @@
 HALF = 14
 UP_LANE = 64
 STRIDE = 136
+FOLD = 2048
 FIRST_ROWS = 32
 MESH = pl.DeviceIdType.MESH
 
@@ -172,12 +173,16 @@
     def _():
         pltpu.make_async_copy(table, own_slots, table_sems.at[0]).start()
 
-    def padded(source, target, count):
-        target[...] = jnp.zeros_like(target)
-
-        @pl.loop(0, count)
-        def _(i):
-            target[i, : source.shape[1], : source.shape[2]] = source[i]
+    def folded(flat, target, count):
+        for start in range(0, U * R, LANES):
+            width = min(LANES, U * R - start)
+            turned = flat[:, start : start + width].astype(jnp.float32).T
+            spread[pl.ds(start, width), :count] = turned
+        for side in range(R):
+            rows = spread[pl.ds(side, U, stride=R), :].T
+            spread[pl.ds(FOLD + side, count, stride=R), :U] = rows[:count]
+        whole = spread[pl.ds(FOLD, count * R), :].astype(jnp.bfloat16)
+        target[...] = whole.reshape(count, R, LANES)
 
     def unfolded(flat, offset, base, count):
         def tile(block, height):
@@ -206,8 +211,9 @@
                 target[base + block] = matrix(block).T.astype(jnp.bfloat16)
 
     spread[...] = jnp.zeros_like(spread)
-    padded(piece_rhs, piece_rhs_pad, slots)
-    padded(right_side, rhs_pad, cells)
+    folded(piece_rhs, piece_rhs_pad, slots)
+    folded(right_side, rhs_pad, cells)
+    spread[...] = jnp.zeros_like(spread)
 
     loads[0].wait()
     unfolded(inverse_flat, 0, 0, cells)
@@ -502,7 +508,7 @@
     states = pl.pallas_call(
         functools.partial(section_kernel, sizes),
         out_shape=jax.ShapeDtypeStruct((cells, R, U), bf16),
-        in_specs=[smem] + [vmem] * 5 + [pl.BlockSpec(memory_space=pl.ANY)] * 3,
+        in_specs=[smem] + [vmem] * 5 + [pl.BlockSpec(memory_space=pltpu.HBM)] * 3,
         out_specs=vmem,
         scratch_shapes=[
             pltpu.VMEM((cells, 2 * U * U), bf16),
@@ -550,8 +556,8 @@
         piece_owner.reshape(1, slots),
         piece_cell.reshape(1, slots),
         piece_up.reshape(1, slots),
-        right_side.reshape(cells, U, R).swapaxes(1, 2),
-        piece_rhs.reshape(slots, U, R).swapaxes(1, 2),
+        right_side.reshape(cells, U * R),
+        piece_rhs.reshape(slots, U * R),
         up_blocks.reshape(cells, 2 * U * U),
         inverses.reshape(cells, U * U),
         piece_blocks.reshape(slots, U * U),

time: 177 us -> 180 us (1.017)
  local copies, waits for them, and re-layouts: 7.3 us -> 9.89 us
    unnamed x16 -> x18, local copies, waits for them, and re-layouts: 4.95 us -> 8.56 us
where the time goes in v5:
time: 180 us; the launch traced here: 179 us
  Pallas kernels  170 us (94%)
  local copies, waits for them, and re-layouts  9.89 us (5%)
    pallas_call x1, Pallas kernels, on_device(): pl.pallas_call(functools.partial(section_kernel, sizes), out_shape=jax.Sh...  170 us
    unnamed x18, local copies, waits for them, and re-layouts  8.56 us

profile of v5, /device:TPU:449, one launch (start us, length us, event | category | flops | bytes accessed | tf_op | source)
XLA Modules:
  0.0 179.4 jit_solution(10390927927518380747)
XLA Ops:
  0.0 0.0 copy-start
  0.0 1.6 copy-done
  1.6 0.0 copy-start.1
  1.6 1.3 copy-done.1
  2.9 0.0 copy-start.2
  2.9 1.2 copy-done.2
  4.1 0.0 copy-start.3
  4.1 0.9 copy-done.3
  5.0 0.0 copy-start.4
  5.0 0.9 copy-done.4
  5.9 0.0 copy-start.5
  5.9 0.7 copy-done.5
  6.6 0.0 copy-start.6
  6.6 0.7 copy-done.6
  7.3 0.0 copy-start.7
  7.3 0.7 copy-done.7
  7.9 0.0 copy-start.8
  7.9 0.7 copy-done.8
  8.6 169.5 %shard_map.91 = bf16[56,16,100]{2,1,0:T(8,128)(2,1)S(1)} custom-call(s32[2,56]{1,0:T(2,128)S(1)} %bitcast.17, s32[1,48]{1,0:T(1,128)S(1)} %bitcast.18, s32[1,48]{1,0:T(1,128)S(1)} %copy-done.7, s32[1,48]{1,0:T(1,128)S(1)} %copy-done.8, bf16[56,1600]{1,0:T(8,128)(2,1)S(1)} %bitcast.15, bf16[48,1600]{1,0:T(8,128)(2,1)S(1)} %bitcast.16, ...), custom_call_target="tpu_custom_call" | custom-call | tf_op jit(solution)/shard_map/pallas_call | solution.py:508
  178.1 0.5 copy.10
  178.6 0.9 copy.11
Async XLA Ops:
  0.0 1.6 copy-start
  1.6 1.3 copy-start.1
  2.9 1.2 copy-start.2
  4.1 0.9 copy-start.3
  5.0 0.9 copy-start.4
  5.9 0.7 copy-start.5
  6.6 0.7 copy-start.6
  7.3 0.7 copy-start.7
  7.9 0.7 copy-start.8
